TPU v7x, 32 devices: a whole 2x2x4 slice. The times are simulated.
32 devices in a mesh: row: 8 (over z, core), col: 4 (over y, x).
Axes of the slice: x: 2, y: 2, z: 4, core: 2. Of those that a mesh axis runs over, the one named last changes fastest.
Arguments:
- features: bfloat16 [32768, 64], P(('col', 'row')), may hold values from -6 to 6
- weight: bfloat16 [64, 256], replicated, may hold values from -0.75 to 0.75
- cotangent: bfloat16 [32768, 256], P(('row', 'col')), may hold values from -6 to 6
- tile_values: bfloat16 [8, 4, 384, 128, 128], P('row', 'col'), may hold values from -0.25 to 0.25
- tile_rows: int32 [8, 4, 384], P('row', 'col'), may hold values from 0 to 31
- tile_cols: int32 [8, 4, 384], P('row', 'col'), may hold values from 0 to 63
- tile_counts: int32 [8, 4], P('row', 'col'), may hold values from 1 to 384, as said below
Outputs:
- activations: bfloat16 [32768, 256], P(('row', 'col'))
- feature_grad: bfloat16 [32768, 64], P(('col', 'row'))
- weight_grad: float32 [64, 256], replicated
Inputs may be any that keep to these rules, and one draw needn't show every extreme that they name: `tile_counts`: each grid block's number of live tile slots; some grid block uses all 384 slots.
All inputs are finite; a program needn't handle non-finite values.
Results may differ from a plain program's by a relative error of at most 0.006.
Values may be sent and summed in bfloat16 or wider, within the bound.
A program may use at most 128 MiB of HBM per device.

v0:
```python
import jax
import jax.numpy as jnp
from jax import lax
from jax.sharding import PartitionSpec as P


def tile_pass(values, targets, picks, live, source, out_rows, transpose, first_tile):
    side = values.shape[1]
    width = source.shape[1]
    block_size = 64
    tiled = source.reshape(-1, side, width)
    out_tiles = out_rows // side
    rounds = (live + block_size - 1) // block_size

    def advance(number, totals):
        first = number * block_size
        block_values = lax.dynamic_slice_in_dim(values, first, block_size, 0)
        target = lax.dynamic_slice_in_dim(targets, first, block_size, 0) - first_tile
        pick = lax.dynamic_slice_in_dim(picks, first, block_size, 0)
        inside = first + jnp.arange(block_size, dtype=jnp.int32) < live
        inside = inside & (target >= 0) & (target < out_tiles)
        target = jnp.clip(target, 0, out_tiles - 1)
        picked = tiled[pick]
        if transpose:
            product = jnp.einsum(
                "tji,tjf->tif", block_values, picked, preferred_element_type=jnp.float32
            )
        else:
            product = jnp.einsum(
                "tij,tjf->tif", block_values, picked, preferred_element_type=jnp.float32
            )
        product = jnp.where(inside[:, None, None], product, 0.0)
        return totals.at[target].add(product)

    start = jnp.zeros((out_tiles, side, width), jnp.float32)
    totals = lax.fori_loop(0, rounds, advance, start)
    return totals.reshape(out_rows, width)


def backward_local(pre, cotangent):
    sigma = jax.nn.sigmoid(pre)
    pre_grad = (cotangent.astype(jnp.float32) * sigma * (1.0 + pre * (1.0 - sigma))).astype(
        jnp.bfloat16
    )
    return pre_grad


def on_device(features, weight, cotangent, tile_values, tile_rows, tile_cols, tile_counts):
    own_rows = features.shape[0]
    values = tile_values[0, 0]
    rows = tile_rows[0, 0]
    cols = tile_cols[0, 0]
    live = tile_counts[0, 0]
    block_rows = own_rows * lax.axis_size("col")
    sources = lax.all_gather(features, "row", axis=0, tiled=True)
    partial_value = tile_pass(values, rows, cols, live, sources, block_rows, False, 0)
    shares = lax.psum_scatter(partial_value, "col", scatter_dimension=0, tiled=True)
    shares_low = shares.astype(jnp.bfloat16)
    pre = jnp.dot(shares_low, weight, preferred_element_type=jnp.float32)
    activations = jax.nn.silu(pre).astype(jnp.bfloat16)
    pre_grad = backward_local(pre, cotangent)
    own_grad = jnp.dot(pre_grad, weight.T, preferred_element_type=jnp.float32).astype(jnp.bfloat16)
    weight_part = jnp.dot(shares_low.T, pre_grad, preferred_element_type=jnp.float32)
    grad_block = lax.all_gather(own_grad, "col", axis=0, tiled=True)
    source_rows = own_rows * lax.axis_size("row")
    grad_partial = tile_pass(values, cols, rows, live, grad_block, source_rows, True, 0)
    feature_grad = lax.psum_scatter(grad_partial, "row", scatter_dimension=0, tiled=True).astype(
        jnp.bfloat16
    )
    weight_grad = lax.psum(weight_part, ("row", "col"))
    return (activations, feature_grad, weight_grad)


def solution(mesh):
    in_specs = (
        P(("col", "row"), None),
        P(),
        P(("row", "col"), None),
        P("row", "col", None, None, None),
        P("row", "col", None),
        P("row", "col", None),
        P("row", "col"),
    )
    out_specs = (P(("row", "col"), None), P(("col", "row"), None), P())
    return jax.shard_map(
        on_device, mesh=mesh, in_specs=in_specs, out_specs=out_specs, check_vma=False
    )
```

profile of v0, /device:TPU:0, one launch (start us, length us, event | category | flops | bytes accessed | tf_op | source)
XLA Modules:
  0.0 411.5 jit_solution(5940420229295411322)
XLA Ops:
  10.0 24.4 %all-gather.2.cloned.1.call-done = bf16[8192,64]{0,1:T(8,128)(2,1)} async-done(((bf16[1024,64]{0,1:T(8,128)(2,1)}), bf16[8192,64]{0,1:T(8,128)(2,1)}) %all-gather.2.cloned.1.call-update) | async-done | bytes 1048592 | tf_op jit(solution)/shard_map/all_gather | solution.py:55
  37.3 72.0 %while.20 = (s32[]{:T(128)}, f32[32,128,64]{1,2,0:T(8,128)S(1)}, s32[]{:T(128)}, s32[384]{0:T(512)S(1)}, s32[]{:T(128)}, /*index=5*/bf16[384,128,128]{2,1,0:T(8,...) while((s32[]{:T(128)}, f32[32,128,64]{1,2,0:T(8,128)S(1)}, ...), condition=%wide.region_2.3_spmd, body=%wide.region_0.2_spmd.sunk | while | flops 135268160 | bytes 14686519 | solution.py:36
  41.9 3.7 fusion.32
  45.6 3.7 scatter_fusion
  53.9 3.7 fusion.32
  57.6 3.7 scatter_fusion
  65.9 3.7 fusion.32
  77.9 3.7 fusion.32
  81.6 3.7 scatter_fusion
  89.9 3.7 fusion.32
  93.6 3.7 scatter_fusion
  101.9 3.7 fusion.32
  105.6 3.7 scatter_fusion
  110.4 26.4 %reduce-scatter.3.cloned.1.call-done = f32[1024,64]{0,1:T(8,128)} async-done(((f32[4096,64]{0,1:T(8,128)}), f32[1024,64]{0,1:T(8,128)}) %reduce-scatter.3.cloned.1.call-update) | async-done | bytes 262160 | tf_op jit(solution)/shard_map/reduce_scatter | solution.py:57
  140.1 9.9 %all_gather.7 = bf16[4096,64]{0,1:T(8,128)(2,1)S(1)} all-gather(bf16[1024,64]{0,1:T(8,128)(2,1)S(1)} %convolution_convert_fusion), channel_id=1, replica_groups=mesh['row'=8,'col'=4] {'col'}, dimensions={0}, use_global_device_ids=true | all-gather | bytes 655360 | tf_op jit(solution)/shard_map/all_gather | solution.py:64
  152.1 89.9 %while.21 = (s32[]{:T(128)}, f32[64,128,64]{1,2,0:T(8,128)}, s32[]{:T(128)}, s32[384]{0:T(512)S(1)}, s32[]{:T(128)}, /*index=5*/bf16[384,128,128]{2,1,0:T(8,128)...) while((s32[]{:T(128)}, f32[64,128,64]{1,2,0:T(8,128)}, ...), condition=%wide.region_6.7_spmd, body=%wide.region_4.6_spmd.sunk | while | flops 135268160 | bytes 14686519 | solution.py:36
  158.0 9.0 %scatter_fusion.1 = f32[64,128,64]{1,2,0:T(8,128)} fusion(f32[64,128,64]{1,2,0:T(8,128)} %get-tuple-element.302, s32[64]{0:T(128)S(1)} %get-tuple-element.251, f32[64,128,64]{1,2,0:T(8,128)S(1)} %fusion.35), kind=kCustom, calls=%fused_computation.3.clone.1 | custom fusion | flops 524288 | bytes 6291712 | tf_op jit(solution)/shard_map/while/body/scatter-add | solution.py:33
  173.0 9.0 %scatter_fusion.1 = f32[64,128,64]{1,2,0:T(8,128)} fusion(f32[64,128,64]{1,2,0:T(8,128)} %get-tuple-element.302, s32[64]{0:T(128)S(1)} %get-tuple-element.251, f32[64,128,64]{1,2,0:T(8,128)S(1)} %fusion.35), kind=kCustom, calls=%fused_computation.3.clone.1 | custom fusion | flops 524288 | bytes 6291712 | tf_op jit(solution)/shard_map/while/body/scatter-add | solution.py:33
  188.0 9.0 %scatter_fusion.1 = f32[64,128,64]{1,2,0:T(8,128)} fusion(f32[64,128,64]{1,2,0:T(8,128)} %get-tuple-element.302, s32[64]{0:T(128)S(1)} %get-tuple-element.251, f32[64,128,64]{1,2,0:T(8,128)S(1)} %fusion.35), kind=kCustom, calls=%fused_computation.3.clone.1 | custom fusion | flops 524288 | bytes 6291712 | tf_op jit(solution)/shard_map/while/body/scatter-add | solution.py:33
  203.0 9.1 %scatter_fusion.1 = f32[64,128,64]{1,2,0:T(8,128)} fusion(f32[64,128,64]{1,2,0:T(8,128)} %get-tuple-element.302, s32[64]{0:T(128)S(1)} %get-tuple-element.251, f32[64,128,64]{1,2,0:T(8,128)S(1)} %fusion.35), kind=kCustom, calls=%fused_computation.3.clone.1 | custom fusion | flops 524288 | bytes 6291712 | tf_op jit(solution)/shard_map/while/body/scatter-add | solution.py:33
  218.1 9.0 %scatter_fusion.1 = f32[64,128,64]{1,2,0:T(8,128)} fusion(f32[64,128,64]{1,2,0:T(8,128)} %get-tuple-element.302, s32[64]{0:T(128)S(1)} %get-tuple-element.251, f32[64,128,64]{1,2,0:T(8,128)S(1)} %fusion.35), kind=kCustom, calls=%fused_computation.3.clone.1 | custom fusion | flops 524288 | bytes 6291712 | tf_op jit(solution)/shard_map/while/body/scatter-add | solution.py:33
  233.0 9.0 %scatter_fusion.1 = f32[64,128,64]{1,2,0:T(8,128)} fusion(f32[64,128,64]{1,2,0:T(8,128)} %get-tuple-element.302, s32[64]{0:T(128)S(1)} %get-tuple-element.251, f32[64,128,64]{1,2,0:T(8,128)S(1)} %fusion.35), kind=kCustom, calls=%fused_computation.3.clone.1 | custom fusion | flops 524288 | bytes 6291712 | tf_op jit(solution)/shard_map/while/body/scatter-add | solution.py:33
  247.0 33.1 %reduce-scatter.5.cloned.1.call-done = f32[1024,64]{0,1:T(8,128)} async-done(((f32[8192,64]{0,1:T(8,128)}), f32[1024,64]{0,1:T(8,128)}) %reduce-scatter.5.cloned.1.call-update) | async-done | bytes 262160 | tf_op jit(solution)/shard_map/reduce_scatter | solution.py:67
  281.8 121.7 %all-reduce.2.cloned.1.call-done = f32[64,256]{1,0:T(8,128)} async-done(((f32[64,256]{1,0:T(8,128)}), f32[64,256]{1,0:T(8,128)}) %all-reduce.2.cloned.1.call-update) | async-done | bytes 65552 | tf_op jit(solution)/shard_map/psum | solution.py:70
  (86 shorter events, 86.1 us)
Async XLA Ops:
  7.2 129.7 %copy-start = (bf16[64,256]{1,0:T(8,128)(2,1)S(1)}, bf16[64,256]{1,0:T(8,128)(2,1)}, u32[]{:S(2)}) copy-start(bf16[64,256]{1,0:T(8,128)(2,1)} %param.12) | copy-start | bytes 98308
  7.2 27.3 %all-gather.2.cloned.1.call-start = ((), (), s32[]{:S(2)}) async-start(), calls=%async_computation.2 | async-start | bytes 1179648 | tf_op jit(solution)/shard_map/all_gather | solution.py:55
  7.9 128.9 %reduce-scatter.3.cloned.1.call-start = ((), (), s32[]{:S(2)}) async-start(), calls=%async_computation.3 | async-start | bytes 1310720 | tf_op jit(solution)/shard_map/reduce_scatter | solution.py:57
  109.3 27.5 %copy-start.4 = (bf16[1024,256]{1,0:T(8,128)(2,1)S(1)}, bf16[1024,256]{1,0:T(8,128)(2,1)}, u32[]{:S(2)}) copy-start(bf16[1024,256]{1,0:T(8,128)(2,1)} %param.13) | copy-start | bytes 1572868
  110.4 169.8 %reduce-scatter.5.cloned.1.call-start = ((), (), s32[]{:S(2)}) async-start(), calls=%async_computation.4 | async-start | bytes 2359296 | tf_op jit(solution)/shard_map/reduce_scatter | solution.py:67
  139.3 0.8 copy-start.1
  245.1 1.0 copy-start.2
  245.1 1.1 copy-start.3
  245.1 158.4 %all-reduce.2.cloned.1.call-start = ((), (), s32[]{:S(2)}) async-start(), calls=%async_computation.5 | async-start | bytes 131072 | tf_op jit(solution)/shard_map/psum | solution.py:70
Sparse Core Ops, SparseCore 0:
  9.6 24.7 all-gather.1
  110.5 26.2 reduce-scatter.2
  245.2 34.8 reduce-scatter.4
  287.1 116.3 all-reduce.1
where the time goes:
time: 416 us; the launch traced here: 411 us
  waiting for transfers between devices  206 us (50%)
  other arithmetic  89.1 us (21%)
  local copies, waits for them, and re-layouts  47.3 us (11%)
  matrix products  43.9 us (11%)
  between operations  14.5 us (3%)
  blocking collectives  9.95 us (2%)
    psum x1, waiting for transfers between devices, on_device(): weight_grad = lax.psum(weight_part, ('row', 'col'))  122 us
    scatter-add x12, other arithmetic, advance(): return totals.at[target].add(product)  76.4 us
    gather x12, local copies, waits for them, and re-layouts, advance(): picked = tiled[pick]  35.2 us
    reduce_scatter x1, waiting for transfers between devices, on_device(): lax.psum_scatter(grad_partial, 'row', scatter_dimension=0, tiled=True)  33.1 us
    reduce_scatter x1, waiting for transfers between devices, on_device(): lax.psum_scatter(partial_value, 'col', scatter_dimension=0, tiled=True)  26.4 us
    all_gather x1, waiting for transfers between devices, on_device(): sources = lax.all_gather(features, 'row', axis=0, tiled=True)  24.4 us
    dot_general x6, matrix products, advance(): jnp.einsum('tij,tjf->tif', block_values, picked, preferred_element_type=j...  22.3 us
    dot_general x6, matrix products, advance(): jnp.einsum('tji,tjf->tif', block_values, picked, preferred_element_type=j...  18 us
  transfers between devices with their start and end apart: 4, of which 4 were waited for; matrix products, arithmetic and copies ran while one was open for 1% of the time, Pallas kernels for 0%

commit v1 on v0

v1 whole, which is shorter than its diff:
```python
import functools

import jax
import jax.numpy as jnp
from jax import lax
from jax.experimental import pallas as pl
from jax.experimental.pallas import tpu as pltpu
from jax.sharding import PartitionSpec as P

MESH = pl.DeviceIdType.MESH
F32 = jnp.float32
BF16 = jnp.bfloat16
VMEM_LIMIT = 40 * 1024 * 1024


def dot(a, b, contract_a, contract_b):
    return lax.dot_general(
        a, b, (((contract_a,), (contract_b,)), ((), ())), preferred_element_type=F32
    )


def greet(peers):
    barrier = pltpu.get_barrier_semaphore()
    for peer in peers:
        pl.semaphore_signal(barrier, inc=1, device_id=peer, device_id_type=MESH)
    return lambda: pl.semaphore_wait(barrier, len(peers))


def remote(src, dst, send_sem, recv_sem, peer):
    return pltpu.make_async_remote_copy(
        src_ref=src,
        dst_ref=dst,
        send_sem=send_sem,
        recv_sem=recv_sem,
        device_id=peer,
        device_id_type=MESH,
    )


def gather_kernel(n_row, f_ref, out_ref, own, local_sem, send_sem, recv_sem):
    chips = n_row // 2
    me = lax.axis_index("row")
    chip, core = me // 2, me % 2
    partner = {"row": chip * 2 + 1 - core}
    lane = [{"row": lax.rem(chip + d, chips) * 2 + core} for d in range(1, chips)]
    ready = greet(lane + [partner])
    tiles = own.shape[0]
    for t in range(tiles):
        own[t] = f_ref[t * 128 : (t + 1) * 128, :].astype(F32).T.astype(BF16)
    keep = pltpu.make_async_copy(own, out_ref.at[me], local_sem)
    keep.start()
    ready()
    copies = []
    for d in range(1, chips):
        copies.append(remote(own, out_ref.at[me], send_sem.at[d - 1], recv_sem.at[d - 1], lane[d - 1]))
    copies.append(remote(own, out_ref.at[me], send_sem.at[chips - 1], recv_sem.at[chips - 1], partner))
    for copy in copies:
        copy.start()
    for d in range(1, chips):
        came = lax.rem(chip + chips - d, chips) * 2 + core
        remote(own, out_ref.at[came], send_sem.at[d - 1], recv_sem.at[d - 1], partner).wait_recv()
        k = chips - 1 + d
        copy = remote(out_ref.at[came], out_ref.at[came], send_sem.at[k], recv_sem.at[k], partner)
        copy.start()
        copies.append(copy)
    for d in range(chips):
        came = lax.rem(chip + chips - d, chips) * 2 + 1 - core
        k = chips - 1 + d
        remote(own, out_ref.at[came], send_sem.at[k], recv_sem.at[k], partner).wait_recv()
    for copy in copies:
        copy.wait_send()
    keep.wait()


def gather_features(features, n_row):
    rows, width = features.shape
    tiles = rows // 128
    chips = n_row // 2
    return pl.pallas_call(
        functools.partial(gather_kernel, n_row),
        out_shape=jax.ShapeDtypeStruct((n_row, tiles, width, 128), BF16),
        in_specs=[pl.BlockSpec(memory_space=pltpu.VMEM)],
        out_specs=pl.BlockSpec(memory_space=pl.ANY),
        scratch_shapes=[
            pltpu.VMEM((tiles, width, 128), BF16),
            pltpu.SemaphoreType.DMA,
            pltpu.SemaphoreType.DMA((2 * chips - 1,)),
            pltpu.SemaphoreType.DMA((2 * chips - 1,)),
        ],
        compiler_params=pltpu.CompilerParams(
            collective_id=0, has_side_effects=True, vmem_limit_bytes=VMEM_LIMIT
        ),
        name="gather_features",
    )(features)


def tile_kernel(
    transpose, group, live_ref, targets_ref, picks_ref, values_ref, source_ref, out_ref, acc
):
    step = pl.program_id(0)
    per_step = values_ref.shape[0]
    n_targets = out_ref.shape[0]
    live = live_ref[0]

    @pl.when(step == 0)
    def _():
        acc[...] = jnp.zeros_like(acc)

    def body(g, carry):
        for u in range(group):
            local = g * group + u
            slot = step * per_step + local
            pick = picks_ref[slot]
            target = jnp.where(slot < live, targets_ref[slot], n_targets)
            product = dot(source_ref[pick], values_ref[local], 1, 0 if transpose else 1)
            acc[target] += product
        return carry

    left = live - step * per_step
    groups = jnp.clip((left + group - 1) // group, 0, per_step // group)
    lax.fori_loop(0, groups, body, 0)

    @pl.when(step == pl.num_programs(0) - 1)
    def _():
        out_ref[...] = acc[0:n_targets].astype(BF16)


def tile_pass(values, targets, picks, live, source, n_targets, transpose):
    slots, side, _ = values.shape
    n_sources, width, _ = source.shape
    per_step, group = 48, 16
    whole = pl.BlockSpec(memory_space=pltpu.SMEM)
    return pl.pallas_call(
        functools.partial(tile_kernel, transpose, group),
        out_shape=jax.ShapeDtypeStruct((n_targets, width, side), BF16),
        grid=(slots // per_step,),
        in_specs=[
            whole,
            whole,
            whole,
            pl.BlockSpec((per_step, side, side), lambda i: (i, 0, 0)),
            pl.BlockSpec((n_sources, width, side), lambda i: (0, 0, 0)),
        ],
        out_specs=pl.BlockSpec((n_targets, width, side), lambda i: (0, 0, 0)),
        scratch_shapes=[pltpu.VMEM((n_targets + 1, width, side), F32)],
        compiler_params=pltpu.CompilerParams(vmem_limit_bytes=VMEM_LIMIT),
        cost_estimate=pl.CostEstimate(
            flops=2 * slots * side * side * width,
            bytes_accessed=2 * slots * side * side,
            transcendentals=0,
        ),
        name="tiles_backward" if transpose else "tiles_forward",
    )(live, targets, picks, values, source)


def node_kernel(
    n_row, n_col,
    part_ref, weight_ref, cot_ref,
    act_ref, grads_ref, chunk_ref,
    came, own_grad, wgrad, wcame,
    local_sem, a_send, a_recv, g_send, g_recv, w_send, w_recv,
):
    row, col = lax.axis_index("row"), lax.axis_index("col")
    across = [{"col": lax.rem(col + d, n_col)} for d in range(1, n_col)]
    along = [lax.rem(row + d, n_row) for d in range(1, n_row)]
    ready = greet(across + [{"row": r} for r in along])
    ready()
    copies = []
    for d in range(1, n_col):
        target = lax.rem(col + d, n_col)
        copies.append(remote(part_ref.at[target], came.at[d - 1], a_send.at[d - 1], a_recv.at[d - 1], across[d - 1]))
    for copy in copies:
        copy.start()
    for copy in copies:
        copy.wait_recv()
    tiles = own_grad.shape[0]
    weight = weight_ref[...]
    total = None
    for t in range(tiles):
        agg = part_ref[col, t].astype(F32)
        for d in range(1, n_col):
            agg += came[d - 1, t].astype(F32)
        low = agg.astype(BF16)
        nodes = slice(t * 128, (t + 1) * 128)
        pre = jnp.dot(agg.T.astype(BF16), weight, preferred_element_type=F32)
        sigma = 1.0 / (1.0 + jnp.exp(-pre))
        act_ref[nodes, :] = (pre * sigma).astype(BF16)
        cot = cot_ref[nodes, :].astype(F32)
        pre_grad = (cot * sigma * (1.0 + pre * (1.0 - sigma))).astype(BF16)
        own_grad[t] = dot(weight, pre_grad, 1, 1).astype(BF16)
        term = jnp.dot(low, pre_grad, preferred_element_type=F32)
        total = term if total is None else total + term
    keep = pltpu.make_async_copy(own_grad, grads_ref.at[col], local_sem)
    keep.start()
    for d in range(1, n_col):
        copy = remote(own_grad, grads_ref.at[col], g_send.at[d - 1], g_recv.at[d - 1], across[d - 1])
        copy.start()
        copies.append(copy)
    depth = wgrad.shape[1]
    for r in range(n_row):
        wgrad[r] = total[r * depth : (r + 1) * depth]
    w_copies = []
    for d in range(1, n_row):
        r = along[d - 1]
        copy = remote(wgrad.at[r], wcame.at[d - 1], w_send.at[d - 1], w_recv.at[d - 1], {"row": r})
        copy.start()
        w_copies.append(copy)
    for copy in w_copies:
        copy.wait_recv()
    chunk = wgrad[row]
    for d in range(1, n_row):
        chunk += wcame[d - 1]
    chunk_ref[...] = chunk
    for d in range(1, n_col):
        source = lax.rem(col + n_col - d, n_col)
        remote(own_grad, grads_ref.at[source], g_send.at[d - 1], g_recv.at[d - 1], across[d - 1]).wait_recv()
    for copy in copies + w_copies:
        copy.wait_send()
    keep.wait()


def node_step(part, weight, cotangent, n_row, n_col):
    _, tiles, width, side = part.shape
    hidden = weight.shape[1]
    depth = width // n_row
    vmem = pl.BlockSpec(memory_space=pltpu.VMEM)
    dma = pltpu.SemaphoreType.DMA
    return pl.pallas_call(
        functools.partial(node_kernel, n_row, n_col),
        out_shape=(
            jax.ShapeDtypeStruct(cotangent.shape, BF16),
            jax.ShapeDtypeStruct(part.shape, BF16),
            jax.ShapeDtypeStruct((depth, hidden), F32),
        ),
        in_specs=[vmem, vmem, vmem],
        out_specs=(vmem, pl.BlockSpec(memory_space=pl.ANY), vmem),
        scratch_shapes=[
            pltpu.VMEM((n_col - 1, tiles, width, side), BF16),
            pltpu.VMEM((tiles, width, side), BF16),
            pltpu.VMEM((n_row, depth, hidden), F32),
            pltpu.VMEM((n_row - 1, depth, hidden), F32),
            dma,
            dma((n_col - 1,)),
            dma((n_col - 1,)),
            dma((n_col - 1,)),
            dma((n_col - 1,)),
            dma((n_row - 1,)),
            dma((n_row - 1,)),
        ],
        compiler_params=pltpu.CompilerParams(
            collective_id=1, has_side_effects=True, vmem_limit_bytes=VMEM_LIMIT
        ),
        name="node_step",
    )(part, weight, cotangent)


def scatter_kernel(
    n_row, n_col,
    part_ref, chunk_ref,
    out_ref, wgrad_ref,
    other, chip_sum, came, wcols, wsum,
    p_send, p_recv, l_send, l_recv, c_send, c_recv, w_send, w_recv,
):
    chips = n_row // 2
    row, col = lax.axis_index("row"), lax.axis_index("col")
    chip, core = row // 2, row % 2
    partner = {"row": chip * 2 + 1 - core}
    along = [lax.rem(row + d, n_row) for d in range(1, n_row)]
    across = [{"col": lax.rem(col + d, n_col)} for d in range(1, n_col)]
    ready = greet([{"row": r} for r in along] + across)
    ready()
    copies = []
    order = list(range(1, chips)) + [0]
    pairs = []
    for d in order:
        k = lax.rem(chip + d, chips)
        copy = remote(part_ref.at[k * 2 + 1 - core], other.at[d], p_send.at[d], p_recv.at[d], partner)
        copy.start()
        pairs.append(copy)
    for d in range(1, n_col):
        copy = remote(chunk_ref, wcols.at[col], c_send.at[d - 1], c_recv.at[d - 1], across[d - 1])
        copy.start()
        copies.append(copy)
    wcols[col] = chunk_ref[...]
    lanes = []
    for i, d in enumerate(order):
        pairs[i].wait_recv()
        if d == 0:
            continue
        k = lax.rem(chip + d, chips)
        chip_sum[d - 1] = (part_ref[k * 2 + core].astype(F32) + other[d].astype(F32)).astype(BF16)
        copy = remote(chip_sum.at[d - 1], came.at[d - 1], l_send.at[d - 1], l_recv.at[d - 1], {"row": k * 2 + core})
        copy.start()
        lanes.append(copy)
    for d in range(1, n_col):
        source = lax.rem(col + n_col - d, n_col)
        remote(chunk_ref, wcols.at[source], c_send.at[d - 1], c_recv.at[d - 1], across[d - 1]).wait_recv()
    total = wcols[0]
    for c in range(1, n_col):
        total += wcols[c]
    wsum[...] = total
    wgrad_ref[row] = total
    for d in range(1, n_row):
        copy = remote(wsum, wgrad_ref.at[row], w_send.at[d - 1], w_recv.at[d - 1], {"row": along[d - 1]})
        copy.start()
        copies.append(copy)
    for copy in lanes:
        copy.wait_recv()
    for t in range(out_ref.shape[0]):
        block = part_ref[row, t].astype(F32) + other[0, t].astype(F32)
        for d in range(1, chips):
            block += came[d - 1, t].astype(F32)
        out_ref[t] = block.astype(BF16)
    for d in range(1, n_row):
        source = lax.rem(row + n_row - d, n_row)
        remote(wsum, wgrad_ref.at[source], w_send.at[d - 1], w_recv.at[d - 1], partner).wait_recv()
    for copy in copies + pairs + lanes:
        copy.wait_send()


def scatter_step(part, chunk, n_row, n_col):
    _, tiles, width, side = part.shape
    depth, hidden = chunk.shape
    chips = n_row // 2
    vmem = pl.BlockSpec(memory_space=pltpu.VMEM)
    dma = pltpu.SemaphoreType.DMA
    return pl.pallas_call(
        functools.partial(scatter_kernel, n_row, n_col),
        out_shape=(
            jax.ShapeDtypeStruct((tiles, width, side), BF16),
            jax.ShapeDtypeStruct((n_row, depth, hidden), F32),
        ),
        in_specs=[vmem, vmem],
        out_specs=(vmem, vmem),
        scratch_shapes=[
            pltpu.VMEM((chips, tiles, width, side), BF16),
            pltpu.VMEM((chips - 1, tiles, width, side), BF16),
            pltpu.VMEM((chips - 1, tiles, width, side), BF16),
            pltpu.VMEM((n_col, depth, hidden), F32),
            pltpu.VMEM((depth, hidden), F32),
            dma((chips,)),
            dma((chips,)),
            dma((chips - 1,)),
            dma((chips - 1,)),
            dma((n_col - 1,)),
            dma((n_col - 1,)),
            dma((n_row - 1,)),
            dma((n_row - 1,)),
        ],
        compiler_params=pltpu.CompilerParams(
            collective_id=2, has_side_effects=True, vmem_limit_bytes=VMEM_LIMIT
        ),
        name="scatter_step",
    )(part, chunk)


def on_device(n_row, n_col, features, weight, cotangent, tile_values, tile_rows, tile_cols, tile_counts):
    own_rows, width = features.shape
    tiles = own_rows // 128
    values = tile_values[0, 0]
    rows = tile_rows[0, 0]
    cols = tile_cols[0, 0]
    live = tile_counts[0]
    sources = gather_features(features, n_row).reshape(n_row * tiles, width, 128)
    part = tile_pass(values, rows, cols, live, sources, n_col * tiles, False)
    activations, grads, chunk = node_step(
        part.reshape(n_col, tiles, width, 128), weight, cotangent, n_row, n_col
    )
    grads = grads.reshape(n_col * tiles, width, 128)
    grad_part = tile_pass(values, cols, rows, live, grads, n_row * tiles, True)
    out, weight_grad = scatter_step(
        grad_part.reshape(n_row, tiles, width, 128), chunk, n_row, n_col
    )
    feature_grad = jnp.swapaxes(out, 1, 2).reshape(own_rows, width)
    return activations, feature_grad, weight_grad.reshape(weight.shape)


def solution(mesh):
    in_specs = (
        P(("col", "row"), None),
        P(),
        P(("row", "col"), None),
        P("row", "col", None, None, None),
        P("row", "col", None),
        P("row", "col", None),
        P("row", "col"),
    )
    out_specs = (P(("row", "col"), None), P(("col", "row"), None), P())
    return jax.shard_map(
        functools.partial(on_device, mesh.shape["row"], mesh.shape["col"]),
        mesh=mesh,
        in_specs=in_specs,
        out_specs=out_specs,
        check_vma=False,
    )
```

time: 416 us -> 90.7 us (0.22)
  waiting for transfers between devices: 206 us -> 0 us
  other arithmetic: 89.1 us -> 1.4 us
  Pallas kernels: 0 us -> 74.6 us
  matrix products: 43.9 us -> 0 us
  local copies, waits for them, and re-layouts: 47.3 us -> 12.3 us
  between operations: 14.5 us -> 1.43 us
  blocking collectives: 9.95 us -> 0 us
    psum x1 -> x0, waiting for transfers between devices: 122 us -> none  [on_device(): weight_grad = lax.psum(weight_part, ('row', 'col'))]
    scatter-add x12 -> x0, other arithmetic: 76.4 us -> none  [advance(): return totals.at[target].add(product)]
    pallas_call x0 -> x5, Pallas kernels: none -> 74.6 us  [the longest x1 32.1 us: node_step(): pl.pallas_call(functools.partial(node_kernel, n_row, n_col), out_shape=(j...]
    reduce_scatter x2 -> x0, waiting for transfers between devices: 59.5 us -> none  [the longest x1 33.1 us: on_device(): lax.psum_scatter(grad_partial, 'row', scatter_dimension=0, tiled=True)]
    dot_general x15 -> x0, matrix products: 43.9 us -> none  [the longest x6 22.3 us: advance(): jnp.einsum('tij,tjf->tif', block_values, picked, preferred_element_type=j...]
    gather x12 -> x0, local copies, waits for them, and re-layouts: 35.2 us -> none  [advance(): picked = tiled[pick]]
    all_gather x1 -> x0, waiting for transfers between devices: 24.4 us -> none  [on_device(): sources = lax.all_gather(features, 'row', axis=0, tiled=True)]
    all_gather x1 -> x0, blocking collectives: 9.95 us -> none  [on_device(): grad_block = lax.all_gather(own_grad, 'col', axis=0, tiled=True)]
  transfers between devices with their start and end apart: 4 -> 0, of which waited for: 4 -> 0; matrix products, arithmetic and copies ran while one was open for 1% -> 0% of each run, Pallas kernels for 0% -> 0%
where the time goes in v1:
time: 90.7 us; the launch traced here: 89.8 us
  Pallas kernels  74.6 us (82%)
  local copies, waits for them, and re-layouts  12.3 us (14%)
  between operations  1.43 us (2%)
  other arithmetic  1.4 us (2%)
    pallas_call x1, Pallas kernels, node_step(): pl.pallas_call(functools.partial(node_kernel, n_row, n_col), out_shape=(j...  32.1 us
    pallas_call x1, Pallas kernels, scatter_step(): pl.pallas_call(functools.partial(scatter_kernel, n_row, n_col), out_shape...  23.1 us
    pallas_call x1, Pallas kernels, gather_features(): pl.pallas_call(functools.partial(gather_kernel, n_row), out_shape=jax.Sha...  16.4 us
    unnamed x11, local copies, waits for them, and re-layouts  11.6 us
    pallas_call x2, Pallas kernels, tile_pass(): pl.pallas_call(functools.partial(tile_kernel, transpose, group), out_shap...  3.05 us

profile of v1, /device:TPU:0, one launch (start us, length us, event | category | flops | bytes accessed | tf_op | source)
XLA Modules:
  0.0 89.8 jit_solution(14223663273494807837)
XLA Ops:
  0.6 0.0 copy-start.2
  0.6 0.0 copy-start.3
  1.4 0.7 reduce.targets_ref.picks_ref
  2.1 0.7 reduce.1.picks_ref.targets_ref
  2.8 1.1 %copy.11.f_ref = bf16[1024,64]{1,0:T(8,128)(2,1)S(1)} copy(bf16[1024,64]{0,1:T(8,128)(2,1)} %param.7) | data formatting | bytes 262144 | tf_op args[0]
  3.8 16.4 %gather_features.1 = bf16[8,8,64,128]{3,2,1,0:T(8,128)(2,1)S(1)} custom-call(bf16[1024,64]{1,0:T(8,128)(2,1)S(1)} %copy.11.f_ref), custom_call_target="tpu_custom_call" | custom-call | tf_op jit(solution)/shard_map/gather_features/pallas_call | solution.py:79
  20.2 0.0 copy-start
  20.2 4.6 %copy-done = bf16[1,1,384,128,128]{4,3,2,1,0:T(8,128)(2,1)S(1)} copy-done((bf16[1,1,384,128,128]{4,3,2,1,0:T(8,128)(2,1)S(1)}, bf16[1,1,384,128,128]{4,3,2,1,0:T(8,128)(2,1)}, u32[]{:S(2)}) %copy-start) | copy-done | bytes 12582936
  24.8 1.6 %tiles_forward.1 = bf16[32,64,128]{2,1,0:T(8,128)(2,1)S(1)} custom-call(s32[1]{0:T(128)} %bitcast.13.live_ref, s32[384]{0:T(512)S(1)} %reduce.targets_ref.picks_ref, s32[384]{0:T(512)S(1)} %reduce.1.picks_ref.targets_ref, bf16[384,128,128]{2,1,0:T(8,128)(2,1)S(1)} %bitcast.15, bf16[64,64,128]{2,1,0:T(8,128)(2,1)S(1)} %bitcast.17), custom_call_target="tpu_custom_call" | custom-call | flops 805306368 | bytes 12582912 | tf_op jit(solution)/shard_map/tiles_forward/pallas_call | solution.py:133
  26.3 0.0 copy-done.2
  26.4 0.0 copy-done.3
  26.4 32.1 %node_step.1 = (bf16[1024,256]{1,0:T(8,128)(2,1)S(1)}, bf16[4,8,64,128]{3,2,1,0:T(8,128)(2,1)S(1)}, f32[8,256]{1,0:T(8,128)S(1)}) custom-call(bf16[4,8,64,128]{3,2,1,0:T(8,128)(2,1)S(1)} %bitcast.19, bf16[64,256]{1,0:T(8,128)(2,1)S(1)} %copy-done.3, bf16[1024,256]{1,0:T(8,128)(2,1)S(1)} %copy-done.2), custom_call_target="tpu_custom_call" | custom-call | tf_op jit(solution)/shard_map/node_step/pallas_call | solution.py:228
  58.5 0.0 copy-start.1
  58.5 4.6 %copy-done.1 = bf16[1,1,384,128,128]{4,3,2,1,0:T(8,128)(2,1)S(1)} copy-done((bf16[1,1,384,128,128]{4,3,2,1,0:T(8,128)(2,1)S(1)}, bf16[1,1,384,128,128]{4,3,2,1,0:T(8,128)(2,1)}, u32[]{:S(2)}) %copy-start.1) | copy-done | bytes 12582936
  63.1 1.5 %tiles_backward.1 = bf16[64,64,128]{2,1,0:T(8,128)(2,1)S(1)} custom-call(s32[1]{0:T(128)} %bitcast.14.live_ref, s32[384]{0:T(512)S(1)} %reduce.1.picks_ref.targets_ref, s32[384]{0:T(512)S(1)} %reduce.targets_ref.picks_ref, bf16[384,128,128]{2,1,0:T(8,128)(2,1)S(1)} %bitcast.16, bf16[32,64,128]{2,1,0:T(8,128)(2,1)S(1)} %bitcast.20), custom_call_target="tpu_custom_call" | custom-call | flops 805306368 | bytes 12582912 | tf_op jit(solution)/shard_map/tiles_backward/pallas_call | solution.py:133
  64.6 23.1 %scatter_step.1 = (bf16[8,64,128]{2,1,0:T(8,128)(2,1)S(1)}, f32[8,8,256]{2,1,0:T(8,128)S(1)}) custom-call(bf16[8,8,64,128]{3,2,1,0:T(8,128)(2,1)S(1)} %bitcast.18, f32[8,256]{1,0:T(8,128)S(1)} %get-tuple-element.10.chunk_ref), custom_call_target="tpu_custom_call" | custom-call | tf_op jit(solution)/shard_map/scatter_step/pallas_call | solution.py:327
  87.7 0.7 copy_bitcast_fusion
  88.3 0.8 copy.18
  89.1 0.6 copy.19
Async XLA Ops:
  0.6 25.7 %copy-start.2 = (bf16[1024,256]{1,0:T(8,128)(2,1)S(1)}, bf16[1024,256]{1,0:T(8,128)(2,1)}, u32[]{:S(2)}) copy-start(bf16[1024,256]{1,0:T(8,128)(2,1)} %cot_ref.1) | copy-start | bytes 1572868
  0.6 25.7 %copy-start.3 = (bf16[64,256]{1,0:T(8,128)(2,1)S(1)}, bf16[64,256]{1,0:T(8,128)(2,1)}, u32[]{:S(2)}) copy-start(bf16[64,256]{1,0:T(8,128)(2,1)} %weight_ref.1) | copy-start | bytes 98308
  20.2 4.6 %copy-start = (bf16[1,1,384,128,128]{4,3,2,1,0:T(8,128)(2,1)S(1)}, bf16[1,1,384,128,128]{4,3,2,1,0:T(8,128)(2,1)}, u32[]{:S(2)}) copy-start(bf16[1,1,384,128,128]{4,3,2,1,0:T(8,128)(2,1)} %param.10) | copy-start | bytes 37748740
  58.5 4.6 %copy-start.1 = (bf16[1,1,384,128,128]{4,3,2,1,0:T(8,128)(2,1)S(1)}, bf16[1,1,384,128,128]{4,3,2,1,0:T(8,128)(2,1)}, u32[]{:S(2)}) copy-start(bf16[1,1,384,128,128]{4,3,2,1,0:T(8,128)(2,1)} %param.10) | copy-start | bytes 37748740

commit v2 on v1

v2 whole, which is shorter than its diff:
```python
import functools

import jax
import jax.numpy as jnp
from jax import lax
from jax.experimental import pallas as pl
from jax.experimental.pallas import tpu as pltpu
from jax.sharding import PartitionSpec as P

MESH = pl.DeviceIdType.MESH
F32 = jnp.float32
BF16 = jnp.bfloat16
VMEM_LIMIT = 24 * 1024 * 1024
GATHER_VMEM_LIMIT = 39 * 1024 * 1024
PIECES = 2
GROUP = 16


def inside(chip, chips):
    return (chip >= 0) & (chip < chips)


def dot(a, b, contract_a, contract_b):
    return lax.dot_general(
        a, b, (((contract_a,), (contract_b,)), ((), ())), preferred_element_type=F32
    )


def greet(peers):
    barrier = pltpu.get_barrier_semaphore()
    for peer in peers:
        pl.semaphore_signal(barrier, inc=1, device_id=peer, device_id_type=MESH)
    return lambda: pl.semaphore_wait(barrier, len(peers))


def greet_line(chip, core, chips, peers):
    barrier = pltpu.get_barrier_semaphore()
    for peer in peers:
        pl.semaphore_signal(barrier, inc=1, device_id=peer, device_id_type=MESH)
    count = len(peers)
    for sign in (1, -1):
        there = inside(chip + sign, chips)
        count += there.astype(jnp.int32)

        @pl.when(there)
        def _():
            pl.semaphore_signal(
                barrier, inc=1, device_id={"row": (chip + sign) * 2 + core}, device_id_type=MESH
            )

    return lambda: pl.semaphore_wait(barrier, count)


def remote(src, dst, send_sem, recv_sem, peer):
    return pltpu.make_async_remote_copy(
        src_ref=src,
        dst_ref=dst,
        send_sem=send_sem,
        recv_sem=recv_sem,
        device_id=peer,
        device_id_type=MESH,
    )


def gather_kernel(n_row, f_ref, values_ref, out_ref, kept_ref, load_sem, l_send, l_recv, p_send, p_recv):
    chips = n_row // 2
    me = lax.axis_index("row")
    chip, core = me // 2, me % 2
    partner = {"row": chip * 2 + 1 - core}
    tiles = out_ref.shape[1]
    half = tiles // PIECES
    load = pltpu.make_async_copy(values_ref, kept_ref, load_sem)
    load.start()
    ready = greet_line(chip, core, chips, [partner])
    for t in range(tiles):
        out_ref[me, t] = f_ref[:, t * 128 : (t + 1) * 128]
    ready()

    def block(source, q):
        return out_ref.at[source, pl.ds(q * half, half)]

    def lane(side, hop, q, source, sign):
        piece = block(source, q)
        return remote(
            piece, piece, l_send.at[side, hop - 1, q], l_recv.at[side, hop - 1, q],
            {"row": me + 2 * sign},
        )

    def across(side, hop, q, source):
        piece = block(source, q)
        return remote(piece, piece, p_send.at[side, hop, q], p_recv.at[side, hop, q], partner)

    sides = ((0, 1), (1, -1))
    for q in range(PIECES):
        for side, sign in sides:
            @pl.when(inside(chip + sign, chips))
            def _():
                lane(side, 1, q, me, sign).start()
        across(0, 0, q, me).start()
    for hop in range(1, chips):
        for q in range(PIECES):
            for side, sign in sides:
                source = me - 2 * sign * hop
                came = inside(chip - sign * hop, chips)

                @pl.when(came)
                def _():
                    lane(side, hop, q, source, sign).wait_recv()

                if hop + 1 < chips:
                    @pl.when(came & inside(chip + sign, chips))
                    def _():
                        lane(side, hop + 1, q, source, sign).start()

                @pl.when(came)
                def _():
                    across(side, hop, q, source).start()
    for q in range(PIECES):
        across(0, 0, q, chip * 2 + 1 - core).wait_recv()
        across(0, 0, q, me).wait_send()
        for side, sign in sides:
            @pl.when(inside(chip + sign, chips))
            def _():
                lane(side, 1, q, me, sign).wait_send()
    for hop in range(1, chips):
        for q in range(PIECES):
            for side, sign in sides:
                source = me - 2 * sign * hop
                came = inside(chip - sign * hop, chips)

                @pl.when(came)
                def _():
                    across(side, hop, q, (chip - sign * hop) * 2 + 1 - core).wait_recv()
                    across(side, hop, q, source).wait_send()

                if hop + 1 < chips:
                    @pl.when(came & inside(chip + sign, chips))
                    def _():
                        lane(side, hop + 1, q, source, sign).wait_send()
    load.wait()


def gather_features(features, values, n_row):
    width, rows = features.shape
    tiles = rows // 128
    chips = n_row // 2
    vmem = pl.BlockSpec(memory_space=pltpu.VMEM)
    dma = pltpu.SemaphoreType.DMA
    return pl.pallas_call(
        functools.partial(gather_kernel, n_row),
        out_shape=(
            jax.ShapeDtypeStruct((n_row, tiles, width, 128), BF16),
            jax.ShapeDtypeStruct(values.shape, BF16),
        ),
        in_specs=[vmem, pl.BlockSpec(memory_space=pl.ANY)],
        out_specs=(vmem, vmem),
        scratch_shapes=[
            dma,
            dma((2, chips - 1, PIECES)),
            dma((2, chips - 1, PIECES)),
            dma((2, chips, PIECES)),
            dma((2, chips, PIECES)),
        ],
        compiler_params=pltpu.CompilerParams(
            collective_id=0, has_side_effects=True, vmem_limit_bytes=GATHER_VMEM_LIMIT
        ),
        name="gather_features",
    )(features, values)


def add_tiles(transpose, live_ref, targets_ref, picks_ref, values_ref, source_ref, acc):
    group = GROUP
    live = live_ref[0, 0]
    spare = acc.shape[0] - 1
    acc[...] = jnp.zeros_like(acc)

    def body(g, carry):
        for u in range(group):
            slot = g * group + u
            pick = picks_ref[0, 0, slot]
            target = jnp.where(slot < live, targets_ref[0, 0, slot], spare)
            product = dot(source_ref[pick], values_ref[slot], 1, 0 if transpose else 1)
            acc[target] += product
        return carry

    groups = (live + group - 1) // group
    lax.fori_loop(0, groups, body, 0)


def forward_kernel(live_ref, rows_ref, cols_ref, values_ref, source_ref, out_ref, acc):
    add_tiles(False, live_ref, rows_ref, cols_ref, values_ref, source_ref, acc)
    out_ref[...] = acc[0 : out_ref.shape[0]].astype(BF16)


def backward_kernel(
    live_ref, rows_ref, cols_ref, values_ref, source_ref, act_ref, out_ref, act_out_ref, sem
):
    write = pltpu.make_async_copy(act_ref, act_out_ref, sem)
    write.start()
    add_tiles(True, live_ref, cols_ref, rows_ref, values_ref, source_ref, out_ref)
    write.wait()


def tile_pass(values, rows, cols, live, source, n_targets, activations=None):
    slots, side, _ = values.shape
    width = source.shape[1]
    smem = pl.BlockSpec(memory_space=pltpu.SMEM)
    vmem = pl.BlockSpec(memory_space=pltpu.VMEM)
    cost = pl.CostEstimate(
        flops=2 * slots * side * side * width,
        bytes_accessed=2 * slots * side * side,
        transcendentals=0,
    )
    params = pltpu.CompilerParams(vmem_limit_bytes=VMEM_LIMIT)
    if activations is None:
        return pl.pallas_call(
            forward_kernel,
            out_shape=jax.ShapeDtypeStruct((n_targets, width, side), BF16),
            in_specs=[smem, smem, smem, vmem, vmem],
            out_specs=vmem,
            scratch_shapes=[pltpu.VMEM((n_targets + 1, width, side), F32)],
            compiler_params=params,
            cost_estimate=cost,
            name="tiles_forward",
        )(live, rows, cols, values, source)
    return pl.pallas_call(
        backward_kernel,
        out_shape=(
            jax.ShapeDtypeStruct((n_targets + 1, width, side), F32),
            jax.ShapeDtypeStruct(activations.shape, BF16),
        ),
        in_specs=[smem, smem, smem, vmem, vmem, vmem],
        out_specs=(vmem, pl.BlockSpec(memory_space=pl.ANY)),
        scratch_shapes=[pltpu.SemaphoreType.DMA],
        compiler_params=params,
        cost_estimate=cost,
        name="tiles_backward",
    )(live, rows, cols, values, source, activations)


def node_kernel(
    n_row, n_col,
    part_ref, weight_ref, cot_ref,
    act_ref, grads_ref, chunk_ref,
    came, wgrad, wcame,
    a_send, a_recv, g_send, g_recv, w_send, w_recv,
):
    row, col = lax.axis_index("row"), lax.axis_index("col")
    across = [{"col": lax.rem(col + d, n_col)} for d in range(1, n_col)]
    along = [lax.rem(row + d, n_row) for d in range(1, n_row)]
    ready = greet(across + [{"row": r} for r in along])
    ready()
    tiles = part_ref.shape[1]
    half = tiles // PIECES
    copies = []
    arrivals = []
    for q in range(PIECES):
        piece = pl.ds(q * half, half)
        for d in range(1, n_col):
            copy = remote(
                part_ref.at[lax.rem(col + d, n_col), piece], came.at[d - 1, piece],
                a_send.at[d - 1, q], a_recv.at[d - 1, q], across[d - 1],
            )
            copy.start()
            copies.append(copy)
            arrivals.append(copy)
    weight = weight_ref[...]
    total = None
    for q in range(PIECES):
        for copy in arrivals[q * (n_col - 1) : (q + 1) * (n_col - 1)]:
            copy.wait_recv()
        for t in range(q * half, (q + 1) * half):
            agg = part_ref[col, t].astype(F32)
            for d in range(1, n_col):
                agg += came[d - 1, t].astype(F32)
            low = agg.astype(BF16)
            nodes = slice(t * 128, (t + 1) * 128)
            pre = jnp.dot(agg.T.astype(BF16), weight, preferred_element_type=F32)
            sigma = 1.0 / (1.0 + jnp.exp(-pre))
            act_ref[nodes, :] = (pre * sigma).astype(BF16)
            cot = cot_ref[nodes, :].astype(F32)
            pre_grad = (cot * sigma * (1.0 + pre * (1.0 - sigma))).astype(BF16)
            grads_ref[col, t] = dot(weight, pre_grad, 1, 1).astype(BF16)
            term = jnp.dot(low, pre_grad, preferred_element_type=F32)
            total = term if total is None else total + term
        mine = grads_ref.at[col, pl.ds(q * half, half)]
        for d in range(1, n_col):
            copy = remote(mine, mine, g_send.at[d - 1, q], g_recv.at[d - 1, q], across[d - 1])
            copy.start()
            copies.append(copy)
    depth = wgrad.shape[1]
    for r in range(n_row):
        wgrad[r] = total[r * depth : (r + 1) * depth]
    w_copies = []
    for d in range(1, n_row):
        r = along[d - 1]
        copy = remote(wgrad.at[r], wcame.at[d - 1], w_send.at[d - 1], w_recv.at[d - 1], {"row": r})
        copy.start()
        w_copies.append(copy)
    for copy in w_copies:
        copy.wait_recv()
    chunk = wgrad[row]
    for d in range(1, n_row):
        chunk += wcame[d - 1]
    chunk_ref[...] = chunk
    for q in range(PIECES):
        for d in range(1, n_col):
            theirs = grads_ref.at[lax.rem(col + n_col - d, n_col), pl.ds(q * half, half)]
            remote(theirs, theirs, g_send.at[d - 1, q], g_recv.at[d - 1, q], across[d - 1]).wait_recv()
    for copy in copies + w_copies:
        copy.wait_send()


def node_step(part, weight, cotangent, n_row, n_col):
    _, tiles, width, side = part.shape
    hidden = weight.shape[1]
    depth = width // n_row
    vmem = pl.BlockSpec(memory_space=pltpu.VMEM)
    dma = pltpu.SemaphoreType.DMA
    return pl.pallas_call(
        functools.partial(node_kernel, n_row, n_col),
        out_shape=(
            jax.ShapeDtypeStruct(cotangent.shape, BF16),
            jax.ShapeDtypeStruct(part.shape, BF16),
            jax.ShapeDtypeStruct((depth, hidden), F32),
        ),
        in_specs=[vmem, vmem, vmem],
        out_specs=(vmem, vmem, vmem),
        scratch_shapes=[
            pltpu.VMEM((n_col - 1, tiles, width, side), BF16),
            pltpu.VMEM((n_row, depth, hidden), F32),
            pltpu.VMEM((n_row - 1, depth, hidden), F32),
            dma((n_col - 1, PIECES)),
            dma((n_col - 1, PIECES)),
            dma((n_col - 1, PIECES)),
            dma((n_col - 1, PIECES)),
            dma((n_row - 1,)),
            dma((n_row - 1,)),
        ],
        compiler_params=pltpu.CompilerParams(
            collective_id=1, has_side_effects=True, vmem_limit_bytes=VMEM_LIMIT
        ),
        name="node_step",
    )(part, weight, cotangent)


def scatter_kernel(
    n_row, n_col,
    part_ref, chunk_ref,
    out_ref, wgrad_ref,
    other, leaving, came, total_ref, wcols, wsum,
    p_send, p_recv, l_send, l_recv, c_send, c_recv, w_send, w_recv,
):
    chips = n_row // 2
    row, col = lax.axis_index("row"), lax.axis_index("col")
    chip, core = row // 2, row % 2
    partner = {"row": chip * 2 + 1 - core}
    along = [lax.rem(row + d, n_row) for d in range(1, n_row)]
    across = [{"col": lax.rem(col + d, n_col)} for d in range(1, n_col)]
    ready = greet([{"row": r} for r in along] + across)
    ready()
    tiles = came.shape[2]
    half = tiles // PIECES
    sides = ((0, 1), (1, -1))
    order = [(side, sign, hop) for hop in range(chips - 1, 0, -1) for side, sign in sides]

    def pair(side, hop, q, to_chip):
        piece = pl.ds(q * half, half)
        first = (to_chip * 2 + 1 - core) * tiles + q * half
        return remote(
            part_ref.at[pl.ds(first, half)], other.at[side, hop, piece],
            p_send.at[side, hop, q], p_recv.at[side, hop, q], partner,
        )

    def lane(side, hop, q, sign):
        piece = pl.ds(q * half, half)
        return remote(
            leaving.at[side, hop - 1, piece], came.at[side, hop - 1, piece],
            l_send.at[side, hop - 1, q], l_recv.at[side, hop - 1, q],
            {"row": row + 2 * sign},
        )

    for side, sign, hop in order:
        @pl.when(inside(chip + sign * hop, chips))
        def _():
            for q in range(PIECES):
                pair(side, hop, q, chip + sign * hop).start()
    for q in range(PIECES):
        pair(0, 0, q, chip).start()
    copies = []
    for d in range(1, n_col):
        copy = remote(chunk_ref, wcols.at[col], c_send.at[d - 1], c_recv.at[d - 1], across[d - 1])
        copy.start()
        copies.append(copy)
    wcols[col] = chunk_ref[...]

    def share_weight_grad():
        for d in range(1, n_col):
            source = lax.rem(col + n_col - d, n_col)
            remote(chunk_ref, wcols.at[source], c_send.at[d - 1], c_recv.at[d - 1], across[d - 1]).wait_recv()
        total = wcols[0]
        for c in range(1, n_col):
            total += wcols[c]
        wsum[...] = total
        wgrad_ref[row] = total
        for d in range(1, n_row):
            copy = remote(wsum, wgrad_ref.at[row], w_send.at[d - 1], w_recv.at[d - 1], {"row": along[d - 1]})
            copy.start()
            copies.append(copy)

    for hop in range(chips - 1, 0, -1):
        for q in range(PIECES):
            for side, sign in sides:
                to_chip = chip + sign * hop
                goes = inside(to_chip, chips)

                @pl.when(goes)
                def _():
                    pair(side, hop, q, to_chip).wait_recv()
                    for t in range(q * half, (q + 1) * half):
                        total_ref[t] = part_ref[(to_chip * 2 + core) * tiles + t] + other[side, hop, t]

                if hop + 1 < chips:
                    @pl.when(goes & inside(chip - sign, chips))
                    def _():
                        lane(side, hop + 1, q, sign).wait_recv()
                        for t in range(q * half, (q + 1) * half):
                            total_ref[t] = total_ref[t] + came[side, hop, t].astype(F32)

                @pl.when(goes)
                def _():
                    for t in range(q * half, (q + 1) * half):
                        leaving[side, hop - 1, t] = total_ref[t].astype(BF16)
                    lane(side, hop, q, sign).start()
        if hop == max(1, chips - 2):
            share_weight_grad()
    for q in range(PIECES):
        pair(0, 0, q, chip).wait_recv()
        for t in range(q * half, (q + 1) * half):
            total_ref[t] = part_ref[row * tiles + t] + other[0, 0, t]
        for side, sign in sides:
            @pl.when(inside(chip - sign, chips))
            def _():
                lane(side, 1, q, sign).wait_recv()
                for t in range(q * half, (q + 1) * half):
                    total_ref[t] = total_ref[t] + came[side, 0, t].astype(F32)
        for t in range(q * half, (q + 1) * half):
            out_ref[:, t * 128 : (t + 1) * 128] = total_ref[t].astype(BF16)
    for d in range(1, n_row):
        source = lax.rem(row + n_row - d, n_row)
        remote(wsum, wgrad_ref.at[source], w_send.at[d - 1], w_recv.at[d - 1], partner).wait_recv()
    for copy in copies:
        copy.wait_send()
    for q in range(PIECES):
        pair(0, 0, q, chip).wait_send()
        for side, sign, hop in order:
            @pl.when(inside(chip + sign * hop, chips))
            def _():
                pair(side, hop, q, chip + sign * hop).wait_send()
                lane(side, hop, q, sign).wait_send()


def scatter_step(part, chunk, tiles, n_row, n_col):
    _, width, side = part.shape
    depth, hidden = chunk.shape
    chips = n_row // 2
    vmem = pl.BlockSpec(memory_space=pltpu.VMEM)
    dma = pltpu.SemaphoreType.DMA
    return pl.pallas_call(
        functools.partial(scatter_kernel, n_row, n_col),
        out_shape=(
            jax.ShapeDtypeStruct((width, tiles * side), BF16),
            jax.ShapeDtypeStruct((n_row, depth, hidden), F32),
        ),
        in_specs=[vmem, vmem],
        out_specs=(vmem, vmem),
        scratch_shapes=[
            pltpu.VMEM((2, chips, tiles, width, side), F32),
            pltpu.VMEM((2, chips - 1, tiles, width, side), BF16),
            pltpu.VMEM((2, chips - 1, tiles, width, side), BF16),
            pltpu.VMEM((tiles, width, side), F32),
            pltpu.VMEM((n_col, depth, hidden), F32),
            pltpu.VMEM((depth, hidden), F32),
            dma((2, chips, PIECES)),
            dma((2, chips, PIECES)),
            dma((2, chips - 1, PIECES)),
            dma((2, chips - 1, PIECES)),
            dma((n_col - 1,)),
            dma((n_col - 1,)),
            dma((n_row - 1,)),
            dma((n_row - 1,)),
        ],
        compiler_params=pltpu.CompilerParams(
            collective_id=2, has_side_effects=True, vmem_limit_bytes=VMEM_LIMIT
        ),
        name="scatter_step",
    )(part, chunk)


def on_device(n_row, n_col, features, weight, cotangent, tile_values, tile_rows, tile_cols, tile_counts):
    own_rows, width = features.shape
    tiles = own_rows // 128
    sources, values = gather_features(features.T, tile_values[0, 0], n_row)
    sources = sources.reshape(n_row * tiles, width, 128)
    part = tile_pass(values, tile_rows, tile_cols, tile_counts, sources, n_col * tiles)
    activations, grads, chunk = node_step(
        part.reshape(n_col, tiles, width, 128), weight, cotangent, n_row, n_col
    )
    grads = grads.reshape(n_col * tiles, width, 128)
    grad_part, activations = tile_pass(
        values, tile_rows, tile_cols, tile_counts, grads, n_row * tiles, activations
    )
    out, weight_grad = scatter_step(grad_part, chunk, tiles, n_row, n_col)
    return activations, out.T, weight_grad.reshape(weight.shape)


def solution(mesh):
    in_specs = (
        P(("col", "row"), None),
        P(),
        P(("row", "col"), None),
        P("row", "col", None, None, None),
        P("row", "col", None),
        P("row", "col", None),
        P("row", "col"),
    )
    out_specs = (P(("row", "col"), None), P(("col", "row"), None), P())
    return jax.shard_map(
        functools.partial(on_device, mesh.shape["row"], mesh.shape["col"]),
        mesh=mesh,
        in_specs=in_specs,
        out_specs=out_specs,
        check_vma=False,
    )
```

time: 90.7 us -> 70.6 us (0.78)
  local copies, waits for them, and re-layouts: 12.3 us -> 2.2 us
  Pallas kernels: 74.6 us -> 66.5 us
  other arithmetic: 1.4 us -> 0 us
    unnamed x11 -> x12, local copies, waits for them, and re-layouts: 11.6 us -> 2.2 us
    pallas_call x1, Pallas kernels: 32.1 us -> 26 us  [node_step(): pl.pallas_call(functools.partial(node_kernel, n_row, n_col), out_shape=(j...]
    pallas_call x1, Pallas kernels: 23.1 us -> 20.9 us  [scatter_step(): pl.pallas_call(functools.partial(scatter_kernel, n_row, n_col), out_shape...]
    unnamed x2 -> x0, other arithmetic: 1.4 us -> none
where the time goes in v2:
time: 70.6 us; the launch traced here: 70.1 us
  Pallas kernels  66.5 us (94%)
  local copies, waits for them, and re-layouts  2.2 us (3%)
  between operations  1.39 us (2%)
    pallas_call x1, Pallas kernels, node_step(): pl.pallas_call(functools.partial(node_kernel, n_row, n_col), out_shape=(j...  26 us
    pallas_call x1, Pallas kernels, scatter_step(): pl.pallas_call(functools.partial(scatter_kernel, n_row, n_col), out_shape...  20.9 us
    pallas_call x1, Pallas kernels, gather_features(): pl.pallas_call(functools.partial(gather_kernel, n_row), out_shape=(jax.Sh...  16.6 us
    unnamed x12, local copies, waits for them, and re-layouts  2.2 us
    pallas_call x1, Pallas kernels, tile_pass(): pl.pallas_call(forward_kernel, out_shape=jax.ShapeDtypeStruct((n_targets,...  1.63 us

profile of v2, /device:TPU:0, one launch (start us, length us, event | category | flops | bytes accessed | tf_op | source)
XLA Modules:
  0.0 70.1 jit_solution(17474978889958992276)
XLA Ops:
  0.6 0.0 copy-start.4
  0.6 0.0 copy-start.3
  1.3 0.0 copy-start.1
  1.3 0.9 %copy-done.1 = bf16[1024,64]{0,1:T(8,128)(2,1)S(1)} copy-done((bf16[1024,64]{0,1:T(8,128)(2,1)S(1)}, bf16[1024,64]{0,1:T(8,128)(2,1)}, u32[]{:S(2)}) %copy-start.1) | copy-done | bytes 131096
  2.2 0.0 copy-start
  2.2 0.0 copy-start.2
  2.2 16.6 %gather_features.1 = (bf16[8,8,64,128]{3,2,1,0:T(8,128)(2,1)S(1)}, bf16[384,128,128]{2,1,0:T(8,128)(2,1)S(1)}) custom-call(bf16[64,1024]{1,0:T(8,128)(2,1)S(1)} %bitcast.10, bf16[384,128,128]{2,1,0:T(8,128)(2,1)} %bitcast.13), custom_call_target="tpu_custom_call" | custom-call | tf_op jit(solution)/shard_map/gather_features/pallas_call | solution.py:149
  18.9 0.0 copy-done.4
  18.9 0.0 copy-done.3
  18.9 1.6 %tiles_forward.1 = bf16[32,64,128]{2,1,0:T(8,128)(2,1)S(1)} custom-call(s32[1,1]{1,0:T(1,128)S(6)} %copy.12.live_ref, s32[1,1,384]{2,1,0:T(1,128)S(1)} %copy-done.3, s32[1,1,384]{2,1,0:T(1,128)S(1)} %copy-done.4, bf16[384,128,128]{2,1,0:T(8,128)(2,1)S(1)} %get-tuple-element.12.values_ref, bf16[64,64,128]{2,1,0:T(8,128)(2,1)S(1)} %bitcast.8), custom_call_target="tpu_custom_call" | custom-call | flops 805306368 | bytes 12582912 | tf_op jit(solution)/shard_map/tiles_forward/pallas_call | solution.py:216
  20.5 0.0 copy-done
  20.5 0.0 copy-done.2
  20.5 26.0 %node_step.1 = (bf16[1024,256]{1,0:T(8,128)(2,1)S(1)}, bf16[4,8,64,128]{3,2,1,0:T(8,128)(2,1)S(1)}, f32[8,256]{1,0:T(8,128)S(1)}) custom-call(bf16[4,8,64,128]{3,2,1,0:T(8,128)(2,1)S(1)} %bitcast.7, bf16[64,256]{1,0:T(8,128)(2,1)S(1)} %copy-done.2, bf16[1024,256]{1,0:T(8,128)(2,1)S(1)} %copy-done), custom_call_target="tpu_custom_call" | custom-call | tf_op jit(solution)/shard_map/node_step/pallas_call | solution.py:320
  46.5 1.4 %tiles_backward.1 = (f32[65,64,128]{2,1,0:T(8,128)S(1)}, bf16[1024,256]{1,0:T(8,128)(2,1)}) custom-call(s32[1,1]{1,0:T(1,128)S(6)} %copy.12.live_ref, s32[1,1,384]{2,1,0:T(1,128)S(1)} %copy-done.3, s32[1,1,384]{2,1,0:T(1,128)S(1)} %copy-done.4, bf16[384,128,128]{2,1,0:T(8,128)(2,1)S(1)} %get-tuple-element.12.values_ref, bf16[32,64,128]{2,1,0:T(8,128)(2,1)S(1)} %bitcast.9, ...), custom_call_target="tpu_custom_call" | custom-call | flops 805306368 | bytes 12582912 | tf_op jit(solution)/shard_map/tiles_backward/pallas_call | solution.py:226
  47.9 20.9 %scatter_step.1 = (bf16[64,1024]{1,0:T(8,128)(2,1)S(1)}, f32[8,8,256]{2,1,0:T(8,128)S(1)}) custom-call(f32[65,64,128]{2,1,0:T(8,128)S(1)} %get-tuple-element.17.part_ref, f32[8,256]{1,0:T(8,128)S(1)} %get-tuple-element.18.chunk_ref), custom_call_target="tpu_custom_call" | custom-call | tf_op jit(solution)/shard_map/scatter_step/pallas_call | solution.py:469
  68.8 0.7 copy.13
  69.4 0.6 copy.14
Async XLA Ops:
  0.6 18.2 %copy-start.4 = (s32[1,1,384]{2,1,0:T(1,128)S(1)}, s32[1,1,384]{2,1,0:T(1,128)}, u32[]{:S(2)}) copy-start(s32[1,1,384]{2,1,0:T(1,128)} %cols_ref.3) | copy-start | bytes 4612
  0.6 18.2 %copy-start.3 = (s32[1,1,384]{2,1,0:T(1,128)S(1)}, s32[1,1,384]{2,1,0:T(1,128)}, u32[]{:S(2)}) copy-start(s32[1,1,384]{2,1,0:T(1,128)} %rows_ref.3) | copy-start | bytes 4612
  1.3 0.9 %copy-start.1 = (bf16[1024,64]{0,1:T(8,128)(2,1)S(1)}, bf16[1024,64]{0,1:T(8,128)(2,1)}, u32[]{:S(2)}) copy-start(bf16[1024,64]{0,1:T(8,128)(2,1)} %param.7) | copy-start | bytes 393220
  2.2 18.3 %copy-start = (bf16[1024,256]{1,0:T(8,128)(2,1)S(1)}, bf16[1024,256]{1,0:T(8,128)(2,1)}, u32[]{:S(2)}) copy-start(bf16[1024,256]{1,0:T(8,128)(2,1)} %cot_ref.1) | copy-start | bytes 1572868
  2.2 18.3 %copy-start.2 = (bf16[64,256]{1,0:T(8,128)(2,1)S(1)}, bf16[64,256]{1,0:T(8,128)(2,1)}, u32[]{:S(2)}) copy-start(bf16[64,256]{1,0:T(8,128)(2,1)} %weight_ref.1) | copy-start | bytes 98308

commit v3 on v2

--- a/solution.py
+++ b/solution.py
@@ -12,8 +12,8 @@
 BF16 = jnp.bfloat16
 VMEM_LIMIT = 24 * 1024 * 1024
 GATHER_VMEM_LIMIT = 39 * 1024 * 1024
-PIECES = 2
-GROUP = 16
+PIECES = 4
+GROUP = 32
 
 
 def inside(chip, chips):
@@ -62,7 +62,7 @@
     )
 
 
-def gather_kernel(n_row, f_ref, values_ref, out_ref, kept_ref, load_sem, l_send, l_recv, p_send, p_recv):
+def gather_kernel(n_row, f_ref, values_ref, out_ref, kept_ref, own_sem, load_sem, l_send, l_recv, p_send, p_recv):
     chips = n_row // 2
     me = lax.axis_index("row")
     chip, core = me // 2, me % 2
@@ -70,10 +70,17 @@
     tiles = out_ref.shape[1]
     half = tiles // PIECES
     load = pltpu.make_async_copy(values_ref, kept_ref, load_sem)
+    ready = greet_line(chip, core, chips, [partner])
+    fetches = []
+    for t in range(tiles):
+        fetch = pltpu.make_async_copy(
+            f_ref.at[:, pl.ds(t * 128, 128)], out_ref.at[me, t], own_sem.at[t]
+        )
+        fetch.start()
+        fetches.append(fetch)
     load.start()
-    ready = greet_line(chip, core, chips, [partner])
-    for t in range(tiles):
-        out_ref[me, t] = f_ref[:, t * 128 : (t + 1) * 128]
+    for fetch in fetches:
+        fetch.wait()
     ready()
 
     def block(source, q):
@@ -152,9 +159,10 @@
             jax.ShapeDtypeStruct((n_row, tiles, width, 128), BF16),
             jax.ShapeDtypeStruct(values.shape, BF16),
         ),
-        in_specs=[vmem, pl.BlockSpec(memory_space=pl.ANY)],
+        in_specs=[pl.BlockSpec(memory_space=pl.ANY)] * 2,
         out_specs=(vmem, vmem),
         scratch_shapes=[
+            dma((tiles,)),
             dma,
             dma((2, chips - 1, PIECES)),
             dma((2, chips - 1, PIECES)),
@@ -168,11 +176,12 @@
     )(features, values)
 
 
-def add_tiles(transpose, live_ref, targets_ref, picks_ref, values_ref, source_ref, acc):
+def add_tiles(transpose, live_ref, targets_ref, picks_ref, values_ref, source_ref, even, odd):
     group = GROUP
     live = live_ref[0, 0]
-    spare = acc.shape[0] - 1
-    acc[...] = jnp.zeros_like(acc)
+    spare = even.shape[0] - 1
+    even[...] = jnp.zeros_like(even)
+    odd[...] = jnp.zeros_like(odd)
 
     def body(g, carry):
         for u in range(group):
@@ -180,6 +189,7 @@
             pick = picks_ref[0, 0, slot]
             target = jnp.where(slot < live, targets_ref[0, 0, slot], spare)
             product = dot(source_ref[pick], values_ref[slot], 1, 0 if transpose else 1)
+            acc = odd if u % 2 else even
             acc[target] += product
         return carry
 
@@ -187,17 +197,20 @@
     lax.fori_loop(0, groups, body, 0)
 
 
-def forward_kernel(live_ref, rows_ref, cols_ref, values_ref, source_ref, out_ref, acc):
-    add_tiles(False, live_ref, rows_ref, cols_ref, values_ref, source_ref, acc)
-    out_ref[...] = acc[0 : out_ref.shape[0]].astype(BF16)
+def forward_kernel(live_ref, rows_ref, cols_ref, values_ref, source_ref, out_ref, even, odd):
+    add_tiles(False, live_ref, rows_ref, cols_ref, values_ref, source_ref, even, odd)
+    n = out_ref.shape[0]
+    out_ref[...] = (even[0:n] + odd[0:n]).astype(BF16)
 
 
 def backward_kernel(
-    live_ref, rows_ref, cols_ref, values_ref, source_ref, act_ref, out_ref, act_out_ref, sem
+    live_ref, rows_ref, cols_ref, values_ref, source_ref, act_ref, out_ref, act_out_ref, even, odd, sem
 ):
     write = pltpu.make_async_copy(act_ref, act_out_ref, sem)
     write.start()
-    add_tiles(True, live_ref, cols_ref, rows_ref, values_ref, source_ref, out_ref)
+    add_tiles(True, live_ref, cols_ref, rows_ref, values_ref, source_ref, even, odd)
+    n = out_ref.shape[0]
+    out_ref[...] = even[0:n] + odd[0:n]
     write.wait()
 
 
@@ -212,13 +225,14 @@
         transcendentals=0,
     )
     params = pltpu.CompilerParams(vmem_limit_bytes=VMEM_LIMIT)
+    totals = [pltpu.VMEM((n_targets + 1, width, side), F32)] * 2
     if activations is None:
         return pl.pallas_call(
             forward_kernel,
             out_shape=jax.ShapeDtypeStruct((n_targets, width, side), BF16),
             in_specs=[smem, smem, smem, vmem, vmem],
             out_specs=vmem,
-            scratch_shapes=[pltpu.VMEM((n_targets + 1, width, side), F32)],
+            scratch_shapes=totals,
             compiler_params=params,
             cost_estimate=cost,
             name="tiles_forward",
@@ -226,12 +240,12 @@
     return pl.pallas_call(
         backward_kernel,
         out_shape=(
-            jax.ShapeDtypeStruct((n_targets + 1, width, side), F32),
+            jax.ShapeDtypeStruct((n_targets, width, side), F32),
             jax.ShapeDtypeStruct(activations.shape, BF16),
         ),
         in_specs=[smem, smem, smem, vmem, vmem, vmem],
         out_specs=(vmem, pl.BlockSpec(memory_space=pl.ANY)),
-        scratch_shapes=[pltpu.SemaphoreType.DMA],
+        scratch_shapes=totals + [pltpu.SemaphoreType.DMA],
         compiler_params=params,
         cost_estimate=cost,
         name="tiles_backward",

time: 70.6 us -> 67.3 us (0.953); the launches traced: 70.1 us -> 67.9 us
  Pallas kernels: 66.5 us -> 64.3 us
    pallas_call x1, Pallas kernels: 20.9 us -> 19.9 us  [scatter_step(): pl.pallas_call(functools.partial(scatter_kernel, n_row, n_col), out_shape...]
    pallas_call x1, Pallas kernels: 26 us -> 25.1 us  [node_step(): pl.pallas_call(functools.partial(node_kernel, n_row, n_col), out_shape=(j...]
where the time goes in v3:
time: 67.3 us; the launch traced here: 67.9 us
  Pallas kernels  64.3 us (96%)
  local copies, waits for them, and re-layouts  2.2 us (3%)
  between operations  1.39 us (2%)
    pallas_call x1, Pallas kernels, node_step(): pl.pallas_call(functools.partial(node_kernel, n_row, n_col), out_shape=(j...  25.1 us
    pallas_call x1, Pallas kernels, scatter_step(): pl.pallas_call(functools.partial(scatter_kernel, n_row, n_col), out_shape...  19.9 us
    pallas_call x1, Pallas kernels, gather_features(): pl.pallas_call(functools.partial(gather_kernel, n_row), out_shape=(jax.Sh...  16.1 us
    unnamed x12, local copies, waits for them, and re-layouts  2.2 us
    pallas_call x1, Pallas kernels, tile_pass(): pl.pallas_call(forward_kernel, out_shape=jax.ShapeDtypeStruct((n_targets,...  1.63 us
    pallas_call x1, Pallas kernels, tile_pass(): pl.pallas_call(backward_kernel, out_shape=(jax.ShapeDtypeStruct((n_target...  1.51 us

profile of v3, /device:TPU:0, one launch (start us, length us, event | category | flops | bytes accessed | tf_op | source)
XLA Modules:
  0.0 67.9 jit_solution(12849106601140660398)
XLA Ops:
  0.6 0.0 copy-start.4
  0.6 0.0 copy-start.3
  1.3 0.0 copy-start.1
  1.3 0.9 %copy-done.1 = bf16[1024,64]{0,1:T(8,128)(2,1)S(1)} copy-done((bf16[1024,64]{0,1:T(8,128)(2,1)S(1)}, bf16[1024,64]{0,1:T(8,128)(2,1)}, u32[]{:S(2)}) %copy-start.1) | copy-done | bytes 131096
  2.2 0.0 copy-start
  2.2 0.0 copy-start.2
  2.2 16.1 %gather_features.1 = (bf16[8,8,64,128]{3,2,1,0:T(8,128)(2,1)S(1)}, bf16[384,128,128]{2,1,0:T(8,128)(2,1)S(1)}) custom-call(bf16[64,1024]{1,0:T(8,128)(2,1)S(1)} %bitcast.10, bf16[384,128,128]{2,1,0:T(8,128)(2,1)} %bitcast.13), custom_call_target="tpu_custom_call" | custom-call | tf_op jit(solution)/shard_map/gather_features/pallas_call | solution.py:156
  18.3 0.0 copy-done.4
  18.4 0.0 copy-done.3
  18.4 1.6 %tiles_forward.1 = bf16[32,64,128]{2,1,0:T(8,128)(2,1)S(1)} custom-call(s32[1,1]{1,0:T(1,128)S(6)} %copy.12.live_ref, s32[1,1,384]{2,1,0:T(1,128)S(1)} %copy-done.3, s32[1,1,384]{2,1,0:T(1,128)S(1)} %copy-done.4, bf16[384,128,128]{2,1,0:T(8,128)(2,1)S(1)} %get-tuple-element.12.values_ref, bf16[64,64,128]{2,1,0:T(8,128)(2,1)S(1)} %bitcast.8), custom_call_target="tpu_custom_call" | custom-call | flops 805306368 | bytes 12582912 | tf_op jit(solution)/shard_map/tiles_forward/pallas_call | solution.py:230
  20.0 0.0 copy-done
  20.0 0.0 copy-done.2
  20.0 25.1 %node_step.1 = (bf16[1024,256]{1,0:T(8,128)(2,1)S(1)}, bf16[4,8,64,128]{3,2,1,0:T(8,128)(2,1)S(1)}, f32[8,256]{1,0:T(8,128)S(1)}) custom-call(bf16[4,8,64,128]{3,2,1,0:T(8,128)(2,1)S(1)} %bitcast.7, bf16[64,256]{1,0:T(8,128)(2,1)S(1)} %copy-done.2, bf16[1024,256]{1,0:T(8,128)(2,1)S(1)} %copy-done), custom_call_target="tpu_custom_call" | custom-call | tf_op jit(solution)/shard_map/node_step/pallas_call | solution.py:334
  45.2 1.5 %tiles_backward.1 = (f32[64,64,128]{2,1,0:T(8,128)S(1)}, bf16[1024,256]{1,0:T(8,128)(2,1)}) custom-call(s32[1,1]{1,0:T(1,128)S(6)} %copy.12.live_ref, s32[1,1,384]{2,1,0:T(1,128)S(1)} %copy-done.3, s32[1,1,384]{2,1,0:T(1,128)S(1)} %copy-done.4, bf16[384,128,128]{2,1,0:T(8,128)(2,1)S(1)} %get-tuple-element.12.values_ref, bf16[32,64,128]{2,1,0:T(8,128)(2,1)S(1)} %bitcast.9, ...), custom_call_target="tpu_custom_call" | custom-call | flops 805306368 | bytes 12582912 | tf_op jit(solution)/shard_map/tiles_backward/pallas_call | solution.py:240
  46.7 19.9 %scatter_step.1 = (bf16[64,1024]{1,0:T(8,128)(2,1)S(1)}, f32[8,8,256]{2,1,0:T(8,128)S(1)}) custom-call(f32[64,64,128]{2,1,0:T(8,128)S(1)} %get-tuple-element.17.part_ref, f32[8,256]{1,0:T(8,128)S(1)} %get-tuple-element.18.chunk_ref), custom_call_target="tpu_custom_call" | custom-call | tf_op jit(solution)/shard_map/scatter_step/pallas_call | solution.py:483
  66.6 0.7 copy.13
  67.2 0.6 copy.14
Async XLA Ops:
  0.6 17.7 %copy-start.4 = (s32[1,1,384]{2,1,0:T(1,128)S(1)}, s32[1,1,384]{2,1,0:T(1,128)}, u32[]{:S(2)}) copy-start(s32[1,1,384]{2,1,0:T(1,128)} %cols_ref.3) | copy-start | bytes 4612
  0.6 17.7 %copy-start.3 = (s32[1,1,384]{2,1,0:T(1,128)S(1)}, s32[1,1,384]{2,1,0:T(1,128)}, u32[]{:S(2)}) copy-start(s32[1,1,384]{2,1,0:T(1,128)} %rows_ref.3) | copy-start | bytes 4612
  1.3 0.9 %copy-start.1 = (bf16[1024,64]{0,1:T(8,128)(2,1)S(1)}, bf16[1024,64]{0,1:T(8,128)(2,1)}, u32[]{:S(2)}) copy-start(bf16[1024,64]{0,1:T(8,128)(2,1)} %param.7) | copy-start | bytes 393220
  2.2 17.8 %copy-start = (bf16[1024,256]{1,0:T(8,128)(2,1)S(1)}, bf16[1024,256]{1,0:T(8,128)(2,1)}, u32[]{:S(2)}) copy-start(bf16[1024,256]{1,0:T(8,128)(2,1)} %cot_ref.1) | copy-start | bytes 1572868
  2.2 17.8 %copy-start.2 = (bf16[64,256]{1,0:T(8,128)(2,1)S(1)}, bf16[64,256]{1,0:T(8,128)(2,1)}, u32[]{:S(2)}) copy-start(bf16[64,256]{1,0:T(8,128)(2,1)} %weight_ref.1) | copy-start | bytes 98308

commit v4 on v3

--- a/solution.py
+++ b/solution.py
@@ -10,10 +10,12 @@
 MESH = pl.DeviceIdType.MESH
 F32 = jnp.float32
 BF16 = jnp.bfloat16
-VMEM_LIMIT = 24 * 1024 * 1024
-GATHER_VMEM_LIMIT = 39 * 1024 * 1024
+VMEM_LIMIT = 14 * 1024 * 1024
+GATHER_VMEM_LIMIT = 20 * 1024 * 1024
 PIECES = 4
 GROUP = 32
+LOADS = 4
+TURNS = 8
 
 
 def inside(chip, chips):
@@ -62,14 +64,18 @@
     )
 
 
-def gather_kernel(n_row, f_ref, values_ref, out_ref, kept_ref, own_sem, load_sem, l_send, l_recv, p_send, p_recv):
+def gather_kernel(n_row, f_ref, values_ref, out_ref, kept_ref, turned_ref, own_sem, load_sem, l_send, l_recv, p_send, p_recv):
     chips = n_row // 2
     me = lax.axis_index("row")
     chip, core = me // 2, me % 2
     partner = {"row": chip * 2 + 1 - core}
     tiles = out_ref.shape[1]
     half = tiles // PIECES
-    load = pltpu.make_async_copy(values_ref, kept_ref, load_sem)
+    slots = kept_ref.shape[0]
+    loads = []
+    for i in range(LOADS):
+        part = pl.ds(i * (slots // LOADS), slots // LOADS)
+        loads.append(pltpu.make_async_copy(values_ref.at[part], kept_ref.at[part], load_sem.at[i]))
     ready = greet_line(chip, core, chips, [partner])
     fetches = []
     for t in range(tiles):
@@ -78,7 +84,8 @@
         )
         fetch.start()
         fetches.append(fetch)
-    load.start()
+    for load in loads:
+        load.start()
     for fetch in fetches:
         fetch.wait()
     ready()
@@ -104,8 +111,21 @@
             def _():
                 lane(side, 1, q, me, sign).start()
         across(0, 0, q, me).start()
+    def turn(i, carry):
+        for u in range(TURNS):
+            turned_ref[i * TURNS + u] = kept_ref[i * TURNS + u].T
+        return carry
+
+    waited = 0
+    rounds = (chips - 1) * PIECES
     for hop in range(1, chips):
         for q in range(PIECES):
+            now = (hop - 1) * PIECES + q
+            first, last = (slots // TURNS * n // rounds for n in (now, now + 1))
+            while waited < LOADS and waited * (slots // LOADS) < last * TURNS:
+                loads[waited].wait()
+                waited += 1
+            lax.fori_loop(first, last, turn, 0)
             for side, sign in sides:
                 source = me - 2 * sign * hop
                 came = inside(chip - sign * hop, chips)
@@ -144,7 +164,6 @@
                     @pl.when(came & inside(chip + sign, chips))
                     def _():
                         lane(side, hop + 1, q, source, sign).wait_send()
-    load.wait()
 
 
 def gather_features(features, values, n_row):
@@ -158,12 +177,13 @@
         out_shape=(
             jax.ShapeDtypeStruct((n_row, tiles, width, 128), BF16),
             jax.ShapeDtypeStruct(values.shape, BF16),
+            jax.ShapeDtypeStruct(values.shape, BF16),
         ),
         in_specs=[pl.BlockSpec(memory_space=pl.ANY)] * 2,
-        out_specs=(vmem, vmem),
+        out_specs=(vmem, vmem, vmem),
         scratch_shapes=[
             dma((tiles,)),
-            dma,
+            dma((LOADS,)),
             dma((2, chips - 1, PIECES)),
             dma((2, chips - 1, PIECES)),
             dma((2, chips, PIECES)),
@@ -176,7 +196,7 @@
     )(features, values)
 
 
-def add_tiles(transpose, live_ref, targets_ref, picks_ref, values_ref, source_ref, even, odd):
+def add_tiles(live_ref, targets_ref, picks_ref, values_ref, source_ref, even, odd):
     group = GROUP
     live = live_ref[0, 0]
     spare = even.shape[0] - 1
@@ -188,7 +208,7 @@
             slot = g * group + u
             pick = picks_ref[0, 0, slot]
             target = jnp.where(slot < live, targets_ref[0, 0, slot], spare)
-            product = dot(source_ref[pick], values_ref[slot], 1, 0 if transpose else 1)
+            product = dot(source_ref[pick], values_ref[slot], 1, 0)
             acc = odd if u % 2 else even
             acc[target] += product
         return carry
@@ -198,7 +218,7 @@
 
 
 def forward_kernel(live_ref, rows_ref, cols_ref, values_ref, source_ref, out_ref, even, odd):
-    add_tiles(False, live_ref, rows_ref, cols_ref, values_ref, source_ref, even, odd)
+    add_tiles(live_ref, rows_ref, cols_ref, values_ref, source_ref, even, odd)
     n = out_ref.shape[0]
     out_ref[...] = (even[0:n] + odd[0:n]).astype(BF16)
 
@@ -208,7 +228,7 @@
 ):
     write = pltpu.make_async_copy(act_ref, act_out_ref, sem)
     write.start()
-    add_tiles(True, live_ref, cols_ref, rows_ref, values_ref, source_ref, even, odd)
+    add_tiles(live_ref, cols_ref, rows_ref, values_ref, source_ref, even, odd)
     n = out_ref.shape[0]
     out_ref[...] = even[0:n] + odd[0:n]
     write.wait()
@@ -255,14 +275,12 @@
 def node_kernel(
     n_row, n_col,
     part_ref, weight_ref, cot_ref,
-    act_ref, grads_ref, chunk_ref,
-    came, wgrad, wcame,
-    a_send, a_recv, g_send, g_recv, w_send, w_recv,
+    act_ref, grads_ref, wgrad_ref,
+    came, a_send, a_recv, g_send, g_recv,
 ):
-    row, col = lax.axis_index("row"), lax.axis_index("col")
+    col = lax.axis_index("col")
     across = [{"col": lax.rem(col + d, n_col)} for d in range(1, n_col)]
-    along = [lax.rem(row + d, n_row) for d in range(1, n_row)]
-    ready = greet(across + [{"row": r} for r in along])
+    ready = greet(across)
     ready()
     tiles = part_ref.shape[1]
     half = tiles // PIECES
@@ -302,26 +320,14 @@
             copy = remote(mine, mine, g_send.at[d - 1, q], g_recv.at[d - 1, q], across[d - 1])
             copy.start()
             copies.append(copy)
-    depth = wgrad.shape[1]
+    depth = wgrad_ref.shape[1]
     for r in range(n_row):
-        wgrad[r] = total[r * depth : (r + 1) * depth]
-    w_copies = []
-    for d in range(1, n_row):
-        r = along[d - 1]
-        copy = remote(wgrad.at[r], wcame.at[d - 1], w_send.at[d - 1], w_recv.at[d - 1], {"row": r})
-        copy.start()
-        w_copies.append(copy)
-    for copy in w_copies:
-        copy.wait_recv()
-    chunk = wgrad[row]
-    for d in range(1, n_row):
-        chunk += wcame[d - 1]
-    chunk_ref[...] = chunk
+        wgrad_ref[r] = total[r * depth : (r + 1) * depth]
     for q in range(PIECES):
         for d in range(1, n_col):
             theirs = grads_ref.at[lax.rem(col + n_col - d, n_col), pl.ds(q * half, half)]
             remote(theirs, theirs, g_send.at[d - 1, q], g_recv.at[d - 1, q], across[d - 1]).wait_recv()
-    for copy in copies + w_copies:
+    for copy in copies:
         copy.wait_send()
 
 
@@ -336,20 +342,16 @@
         out_shape=(
             jax.ShapeDtypeStruct(cotangent.shape, BF16),
             jax.ShapeDtypeStruct(part.shape, BF16),
-            jax.ShapeDtypeStruct((depth, hidden), F32),
+            jax.ShapeDtypeStruct((n_row, depth, hidden), F32),
         ),
         in_specs=[vmem, vmem, vmem],
         out_specs=(vmem, vmem, vmem),
         scratch_shapes=[
             pltpu.VMEM((n_col - 1, tiles, width, side), BF16),
-            pltpu.VMEM((n_row, depth, hidden), F32),
-            pltpu.VMEM((n_row - 1, depth, hidden), F32),
             dma((n_col - 1, PIECES)),
             dma((n_col - 1, PIECES)),
             dma((n_col - 1, PIECES)),
             dma((n_col - 1, PIECES)),
-            dma((n_row - 1,)),
-            dma((n_row - 1,)),
         ],
         compiler_params=pltpu.CompilerParams(
             collective_id=1, has_side_effects=True, vmem_limit_bytes=VMEM_LIMIT
@@ -360,10 +362,10 @@
 
 def scatter_kernel(
     n_row, n_col,
-    part_ref, chunk_ref,
+    part_ref, term_ref,
     out_ref, wgrad_ref,
-    other, leaving, came, total_ref, wcols, wsum,
-    p_send, p_recv, l_send, l_recv, c_send, c_recv, w_send, w_recv,
+    other, leaving, came, total_ref, wrows, wcols, wsum,
+    p_send, p_recv, l_send, l_recv, r_send, r_recv, c_send, c_recv, w_send, w_recv,
 ):
     chips = n_row // 2
     row, col = lax.axis_index("row"), lax.axis_index("col")
@@ -402,16 +404,33 @@
     for q in range(PIECES):
         pair(0, 0, q, chip).start()
     copies = []
-    for d in range(1, n_col):
-        copy = remote(chunk_ref, wcols.at[col], c_send.at[d - 1], c_recv.at[d - 1], across[d - 1])
+    arrivals = []
+    for d in range(1, n_row):
+        copy = remote(
+            term_ref.at[along[d - 1]], wrows.at[d - 1], r_send.at[d - 1], r_recv.at[d - 1],
+            {"row": along[d - 1]},
+        )
         copy.start()
         copies.append(copy)
-    wcols[col] = chunk_ref[...]
-
-    def share_weight_grad():
+        arrivals.append(copy)
+
+    def sum_rows():
+        for copy in arrivals:
+            copy.wait_recv()
+        total = term_ref[row]
+        for d in range(1, n_row):
+            total += wrows[d - 1]
+        wcols[col] = total
         for d in range(1, n_col):
-            source = lax.rem(col + n_col - d, n_col)
-            remote(chunk_ref, wcols.at[source], c_send.at[d - 1], c_recv.at[d - 1], across[d - 1]).wait_recv()
+            mine = wcols.at[col]
+            copy = remote(mine, mine, c_send.at[d - 1], c_recv.at[d - 1], across[d - 1])
+            copy.start()
+            copies.append(copy)
+
+    def sum_cols():
+        for d in range(1, n_col):
+            theirs = wcols.at[lax.rem(col + n_col - d, n_col)]
+            remote(theirs, theirs, c_send.at[d - 1], c_recv.at[d - 1], across[d - 1]).wait_recv()
         total = wcols[0]
         for c in range(1, n_col):
             total += wcols[c]
@@ -446,8 +465,10 @@
                     for t in range(q * half, (q + 1) * half):
                         leaving[side, hop - 1, t] = total_ref[t].astype(BF16)
                     lane(side, hop, q, sign).start()
+        if hop == chips - 1:
+            sum_rows()
         if hop == max(1, chips - 2):
-            share_weight_grad()
+            sum_cols()
     for q in range(PIECES):
         pair(0, 0, q, chip).wait_recv()
         for t in range(q * half, (q + 1) * half):
@@ -474,9 +495,9 @@
                 lane(side, hop, q, sign).wait_send()
 
 
-def scatter_step(part, chunk, tiles, n_row, n_col):
+def scatter_step(part, term, tiles, n_row, n_col):
     _, width, side = part.shape
-    depth, hidden = chunk.shape
+    _, depth, hidden = term.shape
     chips = n_row // 2
     vmem = pl.BlockSpec(memory_space=pltpu.VMEM)
     dma = pltpu.SemaphoreType.DMA
@@ -493,12 +514,15 @@
             pltpu.VMEM((2, chips - 1, tiles, width, side), BF16),
             pltpu.VMEM((2, chips - 1, tiles, width, side), BF16),
             pltpu.VMEM((tiles, width, side), F32),
+            pltpu.VMEM((n_row - 1, depth, hidden), F32),
             pltpu.VMEM((n_col, depth, hidden), F32),
             pltpu.VMEM((depth, hidden), F32),
             dma((2, chips, PIECES)),
             dma((2, chips, PIECES)),
             dma((2, chips - 1, PIECES)),
             dma((2, chips - 1, PIECES)),
+            dma((n_row - 1,)),
+            dma((n_row - 1,)),
             dma((n_col - 1,)),
             dma((n_col - 1,)),
             dma((n_row - 1,)),
@@ -508,23 +532,23 @@
             collective_id=2, has_side_effects=True, vmem_limit_bytes=VMEM_LIMIT
         ),
         name="scatter_step",
-    )(part, chunk)
+    )(part, term)
 
 
 def on_device(n_row, n_col, features, weight, cotangent, tile_values, tile_rows, tile_cols, tile_counts):
     own_rows, width = features.shape
     tiles = own_rows // 128
-    sources, values = gather_features(features.T, tile_values[0, 0], n_row)
+    sources, values, turned = gather_features(features.T, tile_values[0, 0], n_row)
     sources = sources.reshape(n_row * tiles, width, 128)
-    part = tile_pass(values, tile_rows, tile_cols, tile_counts, sources, n_col * tiles)
-    activations, grads, chunk = node_step(
+    part = tile_pass(turned, tile_rows, tile_cols, tile_counts, sources, n_col * tiles)
+    activations, grads, term = node_step(
         part.reshape(n_col, tiles, width, 128), weight, cotangent, n_row, n_col
     )
     grads = grads.reshape(n_col * tiles, width, 128)
     grad_part, activations = tile_pass(
         values, tile_rows, tile_cols, tile_counts, grads, n_row * tiles, activations
     )
-    out, weight_grad = scatter_step(grad_part, chunk, tiles, n_row, n_col)
+    out, weight_grad = scatter_step(grad_part, term, tiles, n_row, n_col)
     return activations, out.T, weight_grad.reshape(weight.shape)
 
 

time: 67.3 us -> 61 us (0.906); the launches traced: 67.9 us -> 60.8 us
  Pallas kernels: 64.3 us -> 57.2 us
    pallas_call x1, Pallas kernels: 25.1 us -> 14.4 us  [node_step(): pl.pallas_call(functools.partial(node_kernel, n_row, n_col), out_shape=(j...]
    pallas_call x1, Pallas kernels: 1.51 us -> 5.34 us  [tile_pass(): pl.pallas_call(backward_kernel, out_shape=(jax.ShapeDtypeStruct((n_target...]
    pallas_call x1, Pallas kernels: 19.9 us -> 16.1 us  [scatter_step(): pl.pallas_call(functools.partial(scatter_kernel, n_row, n_col), out_shape...]
    pallas_call x1, Pallas kernels: 1.63 us -> 4.91 us  [tile_pass(): pl.pallas_call(forward_kernel, out_shape=jax.ShapeDtypeStruct((n_targets,...]
where the time goes in v4:
time: 61 us; the launch traced here: 60.8 us
  Pallas kernels  57.2 us (94%)
  local copies, waits for them, and re-layouts  2.2 us (4%)
  between operations  1.39 us (2%)
    pallas_call x1, Pallas kernels, gather_features(): pl.pallas_call(functools.partial(gather_kernel, n_row), out_shape=(jax.Sh...  16.5 us
    pallas_call x1, Pallas kernels, scatter_step(): pl.pallas_call(functools.partial(scatter_kernel, n_row, n_col), out_shape...  16.1 us
    pallas_call x1, Pallas kernels, node_step(): pl.pallas_call(functools.partial(node_kernel, n_row, n_col), out_shape=(j...  14.4 us
    pallas_call x1, Pallas kernels, tile_pass(): pl.pallas_call(backward_kernel, out_shape=(jax.ShapeDtypeStruct((n_target...  5.34 us
    pallas_call x1, Pallas kernels, tile_pass(): pl.pallas_call(forward_kernel, out_shape=jax.ShapeDtypeStruct((n_targets,...  4.91 us
    unnamed x12, local copies, waits for them, and re-layouts  2.2 us

profile of v4, /device:TPU:0, one launch (start us, length us, event | category | flops | bytes accessed | tf_op | source)
XLA Modules:
  0.0 60.8 jit_solution(16196133909354299340)
XLA Ops:
  0.6 0.0 copy-start.4
  0.6 0.0 copy-start.3
  1.3 0.0 copy-start.1
  1.3 0.9 %copy-done.1 = bf16[1024,64]{0,1:T(8,128)(2,1)S(1)} copy-done((bf16[1024,64]{0,1:T(8,128)(2,1)S(1)}, bf16[1024,64]{0,1:T(8,128)(2,1)}, u32[]{:S(2)}) %copy-start.1) | copy-done | bytes 131096
  2.2 0.0 copy-start
  2.2 0.0 copy-start.2
  2.2 16.5 %gather_features.1 = (bf16[8,8,64,128]{3,2,1,0:T(8,128)(2,1)S(1)}, bf16[384,128,128]{2,1,0:T(8,128)(2,1)S(1)}, bf16[384,128,128]{2,1,0:T(8,128)(2,1)S(1)}) custom-call(bf16[64,1024]{1,0:T(8,128)(2,1)S(1)} %bitcast.10, bf16[384,128,128]{2,1,0:T(8,128)(2,1)} %bitcast.13), custom_call_target="tpu_custom_call" | custom-call | tf_op jit(solution)/shard_map/gather_features/pallas_call | solution.py:175
  18.7 0.0 copy-done.4
  18.8 0.0 copy-done.3
  18.8 4.9 %tiles_forward.1 = bf16[32,64,128]{2,1,0:T(8,128)(2,1)S(1)} custom-call(s32[1,1]{1,0:T(1,128)S(6)} %copy.12.live_ref, s32[1,1,384]{2,1,0:T(1,128)S(1)} %copy-done.3, s32[1,1,384]{2,1,0:T(1,128)S(1)} %copy-done.4, bf16[384,128,128]{2,1,0:T(8,128)(2,1)S(1)} %get-tuple-element.14.values_ref, bf16[64,64,128]{2,1,0:T(8,128)(2,1)S(1)} %bitcast.8), custom_call_target="tpu_custom_call" | custom-call | flops 805306368 | bytes 12582912 | tf_op jit(solution)/shard_map/tiles_forward/pallas_call | solution.py:250
  23.7 0.0 copy-done
  23.7 0.0 copy-done.2
  23.7 14.4 %node_step.1 = (bf16[1024,256]{1,0:T(8,128)(2,1)S(1)}, bf16[4,8,64,128]{3,2,1,0:T(8,128)(2,1)S(1)}, f32[8,8,256]{2,1,0:T(8,128)S(1)}) custom-call(bf16[4,8,64,128]{3,2,1,0:T(8,128)(2,1)S(1)} %bitcast.7, bf16[64,256]{1,0:T(8,128)(2,1)S(1)} %copy-done.2, bf16[1024,256]{1,0:T(8,128)(2,1)S(1)} %copy-done), custom_call_target="tpu_custom_call" | custom-call | tf_op jit(solution)/shard_map/node_step/pallas_call | solution.py:340
  38.1 5.3 %tiles_backward.1 = (f32[64,64,128]{2,1,0:T(8,128)S(1)}, bf16[1024,256]{1,0:T(8,128)(2,1)}) custom-call(s32[1,1]{1,0:T(1,128)S(6)} %copy.12.live_ref, s32[1,1,384]{2,1,0:T(1,128)S(1)} %copy-done.3, s32[1,1,384]{2,1,0:T(1,128)S(1)} %copy-done.4, bf16[384,128,128]{2,1,0:T(8,128)(2,1)S(1)} %get-tuple-element.13.values_ref, bf16[32,64,128]{2,1,0:T(8,128)(2,1)S(1)} %bitcast.9, ...), custom_call_target="tpu_custom_call" | custom-call | flops 805306368 | bytes 12582912 | tf_op jit(solution)/shard_map/tiles_backward/pallas_call | solution.py:260
  43.5 16.1 %scatter_step.1 = (bf16[64,1024]{1,0:T(8,128)(2,1)S(1)}, f32[8,8,256]{2,1,0:T(8,128)S(1)}) custom-call(f32[64,64,128]{2,1,0:T(8,128)S(1)} %get-tuple-element.19.part_ref, f32[8,8,256]{2,1,0:T(8,128)S(1)} %get-tuple-element.20.term_ref), custom_call_target="tpu_custom_call" | custom-call | tf_op jit(solution)/shard_map/scatter_step/pallas_call | solution.py:504
  59.6 0.7 %copy.13 = bf16[1024,64]{0,1:T(8,128)(2,1)} copy(bf16[1024,64]{0,1:T(8,128)(2,1)S(1)} %bitcast.11) | data formatting | bytes 262144
  60.2 0.6 %copy.14 = f32[64,256]{1,0:T(8,128)} copy(f32[64,256]{1,0:T(8,128)S(1)} %bitcast.12) | data formatting | bytes 131072
Async XLA Ops:
  0.6 18.1 %copy-start.4 = (s32[1,1,384]{2,1,0:T(1,128)S(1)}, s32[1,1,384]{2,1,0:T(1,128)}, u32[]{:S(2)}) copy-start(s32[1,1,384]{2,1,0:T(1,128)} %cols_ref.3) | copy-start | bytes 4612
  0.6 18.1 %copy-start.3 = (s32[1,1,384]{2,1,0:T(1,128)S(1)}, s32[1,1,384]{2,1,0:T(1,128)}, u32[]{:S(2)}) copy-start(s32[1,1,384]{2,1,0:T(1,128)} %rows_ref.3) | copy-start | bytes 4612
  1.3 0.9 %copy-start.1 = (bf16[1024,64]{0,1:T(8,128)(2,1)S(1)}, bf16[1024,64]{0,1:T(8,128)(2,1)}, u32[]{:S(2)}) copy-start(bf16[1024,64]{0,1:T(8,128)(2,1)} %param.7) | copy-start | bytes 393220
  2.2 21.5 %copy-start = (bf16[1024,256]{1,0:T(8,128)(2,1)S(1)}, bf16[1024,256]{1,0:T(8,128)(2,1)}, u32[]{:S(2)}) copy-start(bf16[1024,256]{1,0:T(8,128)(2,1)} %cot_ref.1) | copy-start | bytes 1572868
  2.2 21.5 %copy-start.2 = (bf16[64,256]{1,0:T(8,128)(2,1)S(1)}, bf16[64,256]{1,0:T(8,128)(2,1)}, u32[]{:S(2)}) copy-start(bf16[64,256]{1,0:T(8,128)(2,1)} %weight_ref.1) | copy-start | bytes 98308

commit v5 on v4

--- a/solution.py
+++ b/solution.py
@@ -13,7 +13,7 @@
 VMEM_LIMIT = 14 * 1024 * 1024
 GATHER_VMEM_LIMIT = 20 * 1024 * 1024
 PIECES = 4
-GROUP = 32
+GROUP = 64
 LOADS = 4
 TURNS = 8
 
@@ -64,7 +64,7 @@
     )
 
 
-def gather_kernel(n_row, f_ref, values_ref, out_ref, kept_ref, turned_ref, own_sem, load_sem, l_send, l_recv, p_send, p_recv):
+def gather_kernel(n_row, f_ref, values_ref, out_ref, kept_ref, turned_ref, load_sem, l_send, l_recv, p_send, p_recv):
     chips = n_row // 2
     me = lax.axis_index("row")
     chip, core = me // 2, me % 2
@@ -77,17 +77,10 @@
         part = pl.ds(i * (slots // LOADS), slots // LOADS)
         loads.append(pltpu.make_async_copy(values_ref.at[part], kept_ref.at[part], load_sem.at[i]))
     ready = greet_line(chip, core, chips, [partner])
-    fetches = []
-    for t in range(tiles):
-        fetch = pltpu.make_async_copy(
-            f_ref.at[:, pl.ds(t * 128, 128)], out_ref.at[me, t], own_sem.at[t]
-        )
-        fetch.start()
-        fetches.append(fetch)
     for load in loads:
         load.start()
-    for fetch in fetches:
-        fetch.wait()
+    for t in range(tiles):
+        out_ref[me, t] = f_ref[:, t * 128 : (t + 1) * 128]
     ready()
 
     def block(source, q):
@@ -179,10 +172,9 @@
             jax.ShapeDtypeStruct(values.shape, BF16),
             jax.ShapeDtypeStruct(values.shape, BF16),
         ),
-        in_specs=[pl.BlockSpec(memory_space=pl.ANY)] * 2,
+        in_specs=[vmem, pl.BlockSpec(memory_space=pl.ANY)],
         out_specs=(vmem, vmem, vmem),
         scratch_shapes=[
-            dma((tiles,)),
             dma((LOADS,)),
             dma((2, chips - 1, PIECES)),
             dma((2, chips - 1, PIECES)),
@@ -296,6 +288,28 @@
             copy.start()
             copies.append(copy)
             arrivals.append(copy)
+    square = n_col == 4
+    beside = col + 1 - 2 * lax.rem(col, 2)
+    above = lax.rem(col + 2, n_col)
+    opposite = lax.rem(beside + 2, n_col)
+
+    def grads_copy(k, q, source, target):
+        block = grads_ref.at[source, pl.ds(q * half, half)]
+        return remote(block, block, g_send.at[k, q], g_recv.at[k, q], {"col": target})
+
+    def send_grads(k, q, source, target):
+        copy = grads_copy(k, q, source, target)
+        copy.start()
+        copies.append(copy)
+
+    def relay(q):
+        grads_copy(0, q, beside, beside).wait_recv()
+        grads_copy(1, q, above, above).wait_recv()
+        if q % 2 == 0:
+            send_grads(2, q, beside, above)
+        else:
+            send_grads(2, q, above, beside)
+
     weight = weight_ref[...]
     total = None
     for q in range(PIECES):
@@ -315,18 +329,27 @@
             grads_ref[col, t] = dot(weight, pre_grad, 1, 1).astype(BF16)
             term = jnp.dot(low, pre_grad, preferred_element_type=F32)
             total = term if total is None else total + term
-        mine = grads_ref.at[col, pl.ds(q * half, half)]
-        for d in range(1, n_col):
-            copy = remote(mine, mine, g_send.at[d - 1, q], g_recv.at[d - 1, q], across[d - 1])
-            copy.start()
-            copies.append(copy)
+        if square:
+            send_grads(0, q, col, beside)
+            send_grads(1, q, col, above)
+            if q >= 2:
+                relay(q - 2)
+        else:
+            for d in range(1, n_col):
+                send_grads(d - 1, q, col, lax.rem(col + d, n_col))
     depth = wgrad_ref.shape[1]
     for r in range(n_row):
         wgrad_ref[r] = total[r * depth : (r + 1) * depth]
-    for q in range(PIECES):
-        for d in range(1, n_col):
-            theirs = grads_ref.at[lax.rem(col + n_col - d, n_col), pl.ds(q * half, half)]
-            remote(theirs, theirs, g_send.at[d - 1, q], g_recv.at[d - 1, q], across[d - 1]).wait_recv()
+    if square:
+        for q in range(max(0, PIECES - 2), PIECES):
+            relay(q)
+    for q in range(PIECES):
+        if square:
+            grads_copy(2, q, opposite, above).wait_recv()
+        else:
+            for d in range(1, n_col):
+                source = lax.rem(col + n_col - d, n_col)
+                grads_copy(d - 1, q, source, source).wait_recv()
     for copy in copies:
         copy.wait_send()
 

time: 61 us -> 61.6 us (level); the launches traced: 60.8 us -> 62.6 us
  Pallas kernels: 57.2 us -> 59 us
    pallas_call x1, Pallas kernels: 14.4 us -> 18.3 us  [node_step(): pl.pallas_call(functools.partial(node_kernel, n_row, n_col), out_shape=(j...]
    pallas_call x1, Pallas kernels: 5.34 us -> 3.95 us  [tile_pass(): pl.pallas_call(backward_kernel, out_shape=(jax.ShapeDtypeStruct((n_target...]
    pallas_call x1, Pallas kernels: 4.91 us -> 3.55 us  [tile_pass(): pl.pallas_call(forward_kernel, out_shape=jax.ShapeDtypeStruct((n_targets,...]
    pallas_call x1, Pallas kernels: 16.1 us -> 16.8 us  [scatter_step(): pl.pallas_call(functools.partial(scatter_kernel, n_row, n_col), out_shape...]
where the time goes in v5:
time: 61.6 us; the launch traced here: 62.6 us
  Pallas kernels  59 us (96%)
  local copies, waits for them, and re-layouts  2.2 us (4%)
  between operations  1.39 us (2%)
    pallas_call x1, Pallas kernels, node_step(): pl.pallas_call(functools.partial(node_kernel, n_row, n_col), out_shape=(j...  18.3 us
    pallas_call x1, Pallas kernels, scatter_step(): pl.pallas_call(functools.partial(scatter_kernel, n_row, n_col), out_shape...  16.8 us
    pallas_call x1, Pallas kernels, gather_features(): pl.pallas_call(functools.partial(gather_kernel, n_row), out_shape=(jax.Sh...  16.4 us
    pallas_call x1, Pallas kernels, tile_pass(): pl.pallas_call(backward_kernel, out_shape=(jax.ShapeDtypeStruct((n_target...  3.95 us
    pallas_call x1, Pallas kernels, tile_pass(): pl.pallas_call(forward_kernel, out_shape=jax.ShapeDtypeStruct((n_targets,...  3.55 us
    unnamed x12, local copies, waits for them, and re-layouts  2.2 us

profile of v5, /device:TPU:0, one launch (start us, length us, event | category | flops | bytes accessed | tf_op | source)
XLA Modules:
  0.0 62.6 jit_solution(5791796607018133142)
XLA Ops:
  0.6 0.0 copy-start.4
  0.6 0.0 copy-start.3
  1.3 0.0 copy-start.1
  1.3 0.9 %copy-done.1 = bf16[1024,64]{0,1:T(8,128)(2,1)S(1)} copy-done((bf16[1024,64]{0,1:T(8,128)(2,1)S(1)}, bf16[1024,64]{0,1:T(8,128)(2,1)}, u32[]{:S(2)}) %copy-start.1) | copy-done | bytes 131096
  2.2 0.0 copy-start
  2.2 0.0 copy-start.2
  2.2 16.4 %gather_features.1 = (bf16[8,8,64,128]{3,2,1,0:T(8,128)(2,1)S(1)}, bf16[384,128,128]{2,1,0:T(8,128)(2,1)S(1)}, bf16[384,128,128]{2,1,0:T(8,128)(2,1)S(1)}) custom-call(bf16[64,1024]{1,0:T(8,128)(2,1)S(1)} %bitcast.10, bf16[384,128,128]{2,1,0:T(8,128)(2,1)} %bitcast.13), custom_call_target="tpu_custom_call" | custom-call | tf_op jit(solution)/shard_map/gather_features/pallas_call | solution.py:168
  18.7 0.0 copy-done.4
  18.7 0.0 copy-done.3
  18.7 3.6 %tiles_forward.1 = bf16[32,64,128]{2,1,0:T(8,128)(2,1)S(1)} custom-call(s32[1,1]{1,0:T(1,128)S(6)} %copy.12.live_ref, s32[1,1,384]{2,1,0:T(1,128)S(1)} %copy-done.3, s32[1,1,384]{2,1,0:T(1,128)S(1)} %copy-done.4, bf16[384,128,128]{2,1,0:T(8,128)(2,1)S(1)} %get-tuple-element.14.values_ref, bf16[64,64,128]{2,1,0:T(8,128)(2,1)S(1)} %bitcast.8), custom_call_target="tpu_custom_call" | custom-call | flops 805306368 | bytes 12582912 | tf_op jit(solution)/shard_map/tiles_forward/pallas_call | solution.py:242
  22.3 0.0 copy-done
  22.3 0.0 copy-done.2
  22.3 18.3 %node_step.1 = (bf16[1024,256]{1,0:T(8,128)(2,1)S(1)}, bf16[4,8,64,128]{3,2,1,0:T(8,128)(2,1)S(1)}, f32[8,8,256]{2,1,0:T(8,128)S(1)}) custom-call(bf16[4,8,64,128]{3,2,1,0:T(8,128)(2,1)S(1)} %bitcast.7, bf16[64,256]{1,0:T(8,128)(2,1)S(1)} %copy-done.2, bf16[1024,256]{1,0:T(8,128)(2,1)S(1)} %copy-done), custom_call_target="tpu_custom_call" | custom-call | tf_op jit(solution)/shard_map/node_step/pallas_call | solution.py:363
  40.6 3.9 %tiles_backward.1 = (f32[64,64,128]{2,1,0:T(8,128)S(1)}, bf16[1024,256]{1,0:T(8,128)(2,1)}) custom-call(s32[1,1]{1,0:T(1,128)S(6)} %copy.12.live_ref, s32[1,1,384]{2,1,0:T(1,128)S(1)} %copy-done.3, s32[1,1,384]{2,1,0:T(1,128)S(1)} %copy-done.4, bf16[384,128,128]{2,1,0:T(8,128)(2,1)S(1)} %get-tuple-element.13.values_ref, bf16[32,64,128]{2,1,0:T(8,128)(2,1)S(1)} %bitcast.9, ...), custom_call_target="tpu_custom_call" | custom-call | flops 805306368 | bytes 12582912 | tf_op jit(solution)/shard_map/tiles_backward/pallas_call | solution.py:252
  44.6 16.8 %scatter_step.1 = (bf16[64,1024]{1,0:T(8,128)(2,1)S(1)}, f32[8,8,256]{2,1,0:T(8,128)S(1)}) custom-call(f32[64,64,128]{2,1,0:T(8,128)S(1)} %get-tuple-element.19.part_ref, f32[8,8,256]{2,1,0:T(8,128)S(1)} %get-tuple-element.20.term_ref), custom_call_target="tpu_custom_call" | custom-call | tf_op jit(solution)/shard_map/scatter_step/pallas_call | solution.py:527
  61.3 0.7 %copy.13 = bf16[1024,64]{0,1:T(8,128)(2,1)} copy(bf16[1024,64]{0,1:T(8,128)(2,1)S(1)} %bitcast.11) | data formatting | bytes 262144
  62.0 0.6 %copy.14 = f32[64,256]{1,0:T(8,128)} copy(f32[64,256]{1,0:T(8,128)S(1)} %bitcast.12) | data formatting | bytes 131072
Async XLA Ops:
  0.6 18.0 %copy-start.4 = (s32[1,1,384]{2,1,0:T(1,128)S(1)}, s32[1,1,384]{2,1,0:T(1,128)}, u32[]{:S(2)}) copy-start(s32[1,1,384]{2,1,0:T(1,128)} %cols_ref.3) | copy-start | bytes 4612
  0.6 18.0 %copy-start.3 = (s32[1,1,384]{2,1,0:T(1,128)S(1)}, s32[1,1,384]{2,1,0:T(1,128)}, u32[]{:S(2)}) copy-start(s32[1,1,384]{2,1,0:T(1,128)} %rows_ref.3) | copy-start | bytes 4612
  1.3 0.9 %copy-start.1 = (bf16[1024,64]{0,1:T(8,128)(2,1)S(1)}, bf16[1024,64]{0,1:T(8,128)(2,1)}, u32[]{:S(2)}) copy-start(bf16[1024,64]{0,1:T(8,128)(2,1)} %param.7) | copy-start | bytes 393220
  2.2 20.0 %copy-start = (bf16[1024,256]{1,0:T(8,128)(2,1)S(1)}, bf16[1024,256]{1,0:T(8,128)(2,1)}, u32[]{:S(2)}) copy-start(bf16[1024,256]{1,0:T(8,128)(2,1)} %cot_ref.1) | copy-start | bytes 1572868
  2.2 20.0 %copy-start.2 = (bf16[64,256]{1,0:T(8,128)(2,1)S(1)}, bf16[64,256]{1,0:T(8,128)(2,1)}, u32[]{:S(2)}) copy-start(bf16[64,256]{1,0:T(8,128)(2,1)} %weight_ref.1) | copy-start | bytes 98308

commit v6 on v4

--- a/solution.py
+++ b/solution.py
@@ -13,9 +13,9 @@
 VMEM_LIMIT = 14 * 1024 * 1024
 GATHER_VMEM_LIMIT = 20 * 1024 * 1024
 PIECES = 4
-GROUP = 32
+GROUP = 96
 LOADS = 4
-TURNS = 8
+TURNS = 16
 
 
 def inside(chip, chips):
@@ -64,7 +64,7 @@
     )
 
 
-def gather_kernel(n_row, f_ref, values_ref, out_ref, kept_ref, turned_ref, own_sem, load_sem, l_send, l_recv, p_send, p_recv):
+def gather_kernel(n_row, f_ref, values_ref, out_ref, kept_ref, turned_ref, load_sem, l_send, l_recv, p_send, p_recv):
     chips = n_row // 2
     me = lax.axis_index("row")
     chip, core = me // 2, me % 2
@@ -77,17 +77,10 @@
         part = pl.ds(i * (slots // LOADS), slots // LOADS)
         loads.append(pltpu.make_async_copy(values_ref.at[part], kept_ref.at[part], load_sem.at[i]))
     ready = greet_line(chip, core, chips, [partner])
-    fetches = []
-    for t in range(tiles):
-        fetch = pltpu.make_async_copy(
-            f_ref.at[:, pl.ds(t * 128, 128)], out_ref.at[me, t], own_sem.at[t]
-        )
-        fetch.start()
-        fetches.append(fetch)
     for load in loads:
         load.start()
-    for fetch in fetches:
-        fetch.wait()
+    for t in range(tiles):
+        out_ref[me, t] = f_ref[:, t * 128 : (t + 1) * 128]
     ready()
 
     def block(source, q):
@@ -179,10 +172,9 @@
             jax.ShapeDtypeStruct(values.shape, BF16),
             jax.ShapeDtypeStruct(values.shape, BF16),
         ),
-        in_specs=[pl.BlockSpec(memory_space=pl.ANY)] * 2,
+        in_specs=[vmem, pl.BlockSpec(memory_space=pl.ANY)],
         out_specs=(vmem, vmem, vmem),
         scratch_shapes=[
-            dma((tiles,)),
             dma((LOADS,)),
             dma((2, chips - 1, PIECES)),
             dma((2, chips - 1, PIECES)),
@@ -296,6 +288,10 @@
             copy.start()
             copies.append(copy)
             arrivals.append(copy)
+    def grads_copy(k, q, source, target):
+        block = grads_ref.at[source, pl.ds(q * half, half)]
+        return remote(block, block, g_send.at[k, q], g_recv.at[k, q], {"col": target})
+
     weight = weight_ref[...]
     total = None
     for q in range(PIECES):
@@ -315,9 +311,8 @@
             grads_ref[col, t] = dot(weight, pre_grad, 1, 1).astype(BF16)
             term = jnp.dot(low, pre_grad, preferred_element_type=F32)
             total = term if total is None else total + term
-        mine = grads_ref.at[col, pl.ds(q * half, half)]
         for d in range(1, n_col):
-            copy = remote(mine, mine, g_send.at[d - 1, q], g_recv.at[d - 1, q], across[d - 1])
+            copy = grads_copy(d - 1, q, col, lax.rem(col + d, n_col))
             copy.start()
             copies.append(copy)
     depth = wgrad_ref.shape[1]
@@ -325,8 +320,8 @@
         wgrad_ref[r] = total[r * depth : (r + 1) * depth]
     for q in range(PIECES):
         for d in range(1, n_col):
-            theirs = grads_ref.at[lax.rem(col + n_col - d, n_col), pl.ds(q * half, half)]
-            remote(theirs, theirs, g_send.at[d - 1, q], g_recv.at[d - 1, q], across[d - 1]).wait_recv()
+            source = lax.rem(col + n_col - d, n_col)
+            grads_copy(d - 1, q, source, source).wait_recv()
     for copy in copies:
         copy.wait_send()
 

time: 61 us -> 60 us (0.984)
  Pallas kernels: 57.2 us -> 56.4 us
    pallas_call x1, Pallas kernels: 14.4 us -> 16.3 us  [node_step(): pl.pallas_call(functools.partial(node_kernel, n_row, n_col), out_shape=(j...]
    pallas_call x1, Pallas kernels: 5.34 us -> 4.11 us  [tile_pass(): pl.pallas_call(backward_kernel, out_shape=(jax.ShapeDtypeStruct((n_target...]
    pallas_call x1, Pallas kernels: 4.91 us -> 3.69 us  [tile_pass(): pl.pallas_call(forward_kernel, out_shape=jax.ShapeDtypeStruct((n_targets,...]
where the time goes in v6:
time: 60 us; the launch traced here: 59.9 us
  Pallas kernels  56.4 us (94%)
  local copies, waits for them, and re-layouts  2.2 us (4%)
  between operations  1.39 us (2%)
    pallas_call x1, Pallas kernels, node_step(): pl.pallas_call(functools.partial(node_kernel, n_row, n_col), out_shape=(j...  16.3 us
    pallas_call x1, Pallas kernels, scatter_step(): pl.pallas_call(functools.partial(scatter_kernel, n_row, n_col), out_shape...  16.1 us
    pallas_call x1, Pallas kernels, gather_features(): pl.pallas_call(functools.partial(gather_kernel, n_row), out_shape=(jax.Sh...  16.1 us
    pallas_call x1, Pallas kernels, tile_pass(): pl.pallas_call(backward_kernel, out_shape=(jax.ShapeDtypeStruct((n_target...  4.11 us
    pallas_call x1, Pallas kernels, tile_pass(): pl.pallas_call(forward_kernel, out_shape=jax.ShapeDtypeStruct((n_targets,...  3.69 us
    unnamed x12, local copies, waits for them, and re-layouts  2.2 us

profile of v6, /device:TPU:0, one launch (start us, length us, event | category | flops | bytes accessed | tf_op | source)
XLA Modules:
  0.0 59.9 jit_solution(14641671636504347332)
XLA Ops:
  0.6 0.0 copy-start.4
  0.6 0.0 copy-start.3
  1.3 0.0 copy-start.1
  1.3 0.9 %copy-done.1 = bf16[1024,64]{0,1:T(8,128)(2,1)S(1)} copy-done((bf16[1024,64]{0,1:T(8,128)(2,1)S(1)}, bf16[1024,64]{0,1:T(8,128)(2,1)}, u32[]{:S(2)}) %copy-start.1) | copy-done | bytes 131096
  2.2 0.0 copy-start
  2.2 0.0 copy-start.2
  2.2 16.1 %gather_features.1 = (bf16[8,8,64,128]{3,2,1,0:T(8,128)(2,1)S(1)}, bf16[384,128,128]{2,1,0:T(8,128)(2,1)S(1)}, bf16[384,128,128]{2,1,0:T(8,128)(2,1)S(1)}) custom-call(bf16[64,1024]{1,0:T(8,128)(2,1)S(1)} %bitcast.10, bf16[384,128,128]{2,1,0:T(8,128)(2,1)} %bitcast.13), custom_call_target="tpu_custom_call" | custom-call | tf_op jit(solution)/shard_map/gather_features/pallas_call | solution.py:168
  18.3 0.0 copy-done.4
  18.4 0.0 copy-done.3
  18.4 3.7 %tiles_forward.1 = bf16[32,64,128]{2,1,0:T(8,128)(2,1)S(1)} custom-call(s32[1,1]{1,0:T(1,128)S(6)} %copy.12.live_ref, s32[1,1,384]{2,1,0:T(1,128)S(1)} %copy-done.3, s32[1,1,384]{2,1,0:T(1,128)S(1)} %copy-done.4, bf16[384,128,128]{2,1,0:T(8,128)(2,1)S(1)} %get-tuple-element.14.values_ref, bf16[64,64,128]{2,1,0:T(8,128)(2,1)S(1)} %bitcast.8), custom_call_target="tpu_custom_call" | custom-call | flops 805306368 | bytes 12582912 | tf_op jit(solution)/shard_map/tiles_forward/pallas_call | solution.py:242
  22.1 0.0 copy-done
  22.1 0.0 copy-done.2
  22.1 16.3 %node_step.1 = (bf16[1024,256]{1,0:T(8,128)(2,1)S(1)}, bf16[4,8,64,128]{3,2,1,0:T(8,128)(2,1)S(1)}, f32[8,8,256]{2,1,0:T(8,128)S(1)}) custom-call(bf16[4,8,64,128]{3,2,1,0:T(8,128)(2,1)S(1)} %bitcast.7, bf16[64,256]{1,0:T(8,128)(2,1)S(1)} %copy-done.2, bf16[1024,256]{1,0:T(8,128)(2,1)S(1)} %copy-done), custom_call_target="tpu_custom_call" | custom-call | tf_op jit(solution)/shard_map/node_step/pallas_call | solution.py:335
  38.4 4.1 %tiles_backward.1 = (f32[64,64,128]{2,1,0:T(8,128)S(1)}, bf16[1024,256]{1,0:T(8,128)(2,1)}) custom-call(s32[1,1]{1,0:T(1,128)S(6)} %copy.12.live_ref, s32[1,1,384]{2,1,0:T(1,128)S(1)} %copy-done.3, s32[1,1,384]{2,1,0:T(1,128)S(1)} %copy-done.4, bf16[384,128,128]{2,1,0:T(8,128)(2,1)S(1)} %get-tuple-element.13.values_ref, bf16[32,64,128]{2,1,0:T(8,128)(2,1)S(1)} %bitcast.9, ...), custom_call_target="tpu_custom_call" | custom-call | flops 805306368 | bytes 12582912 | tf_op jit(solution)/shard_map/tiles_backward/pallas_call | solution.py:252
  42.5 16.1 %scatter_step.1 = (bf16[64,1024]{1,0:T(8,128)(2,1)S(1)}, f32[8,8,256]{2,1,0:T(8,128)S(1)}) custom-call(f32[64,64,128]{2,1,0:T(8,128)S(1)} %get-tuple-element.19.part_ref, f32[8,8,256]{2,1,0:T(8,128)S(1)} %get-tuple-element.20.term_ref), custom_call_target="tpu_custom_call" | custom-call | tf_op jit(solution)/shard_map/scatter_step/pallas_call | solution.py:499
  58.7 0.7 %copy.13 = bf16[1024,64]{0,1:T(8,128)(2,1)} copy(bf16[1024,64]{0,1:T(8,128)(2,1)S(1)} %bitcast.11) | data formatting | bytes 262144
  59.3 0.6 %copy.14 = f32[64,256]{1,0:T(8,128)} copy(f32[64,256]{1,0:T(8,128)S(1)} %bitcast.12) | data formatting | bytes 131072
Async XLA Ops:
  0.6 17.7 %copy-start.4 = (s32[1,1,384]{2,1,0:T(1,128)S(1)}, s32[1,1,384]{2,1,0:T(1,128)}, u32[]{:S(2)}) copy-start(s32[1,1,384]{2,1,0:T(1,128)} %cols_ref.3) | copy-start | bytes 4612
  0.6 17.7 %copy-start.3 = (s32[1,1,384]{2,1,0:T(1,128)S(1)}, s32[1,1,384]{2,1,0:T(1,128)}, u32[]{:S(2)}) copy-start(s32[1,1,384]{2,1,0:T(1,128)} %rows_ref.3) | copy-start | bytes 4612
  1.3 0.9 %copy-start.1 = (bf16[1024,64]{0,1:T(8,128)(2,1)S(1)}, bf16[1024,64]{0,1:T(8,128)(2,1)}, u32[]{:S(2)}) copy-start(bf16[1024,64]{0,1:T(8,128)(2,1)} %param.7) | copy-start | bytes 393220
  2.2 19.8 %copy-start = (bf16[1024,256]{1,0:T(8,128)(2,1)S(1)}, bf16[1024,256]{1,0:T(8,128)(2,1)}, u32[]{:S(2)}) copy-start(bf16[1024,256]{1,0:T(8,128)(2,1)} %cot_ref.1) | copy-start | bytes 1572868
  2.2 19.8 %copy-start.2 = (bf16[64,256]{1,0:T(8,128)(2,1)S(1)}, bf16[64,256]{1,0:T(8,128)(2,1)}, u32[]{:S(2)}) copy-start(bf16[64,256]{1,0:T(8,128)(2,1)} %weight_ref.1) | copy-start | bytes 98308
